TPU v7x, 32 devices: a whole 2x2x4 slice. The times are simulated.
32 devices in a mesh: dp: 8 (over z, y), tp: 4 (over x, core).
Axes of the slice: x: 2, y: 2, z: 4, core: 2. Of those that a mesh axis runs over, the one named last changes fastest.
Arguments:
- watch_ids: int32 [4096, 50], P(('dp', 'tp')), may hold values from 0 to 131071, as said below
- watch_len: int32 [4096], P(('dp', 'tp')), may hold values from 1 to 50
- search_ids: int32 [4096, 50], P(('dp', 'tp')), may hold values from 0 to 131071, as said below
- search_len: int32 [4096], P(('dp', 'tp')), may hold values from 1 to 50
- search_mask: int32 [4096], P(('dp', 'tp')), may hold values 0 or 1
- positive_ids: int32 [4096], P(('dp', 'tp')), may hold values from 0 to 131071, as said below
- logq_pos: float32 [4096], P(('dp', 'tp')), may hold values from -12 to -9
- negative_ids: int32 [5000], replicated, may hold values from 0 to 131071
- logq_neg: float32 [5000], replicated, may hold values from -12 to -9
- dense_feats: float32 [4096, 128], P(('dp', 'tp')), may hold values from -6 to 6
- watch_table: float32 [131072, 256], P(('dp', 'tp')), may hold values from -6 to 6
- search_table: float32 [131072, 256], P(('dp', 'tp')), may hold values from -6 to 6
- out_table: float32 [131072, 256], P(('dp', 'tp')), may hold values from -0.9 to 0.9
- weight_one: float32 [640, 1024], P(None, 'tp'), may hold values from -0.25 to 0.25
- bias_one: float32 [1024], P('tp'), may hold values from -3 to 3
- weight_two: float32 [1024, 512], P(None, 'tp'), may hold values from -0.1875 to 0.1875
- bias_two: float32 [512], P('tp'), may hold values from -3 to 3
- weight_three: float32 [512, 256], replicated, may hold values from -0.25 to 0.25
- bias_three: float32 [256], replicated, may hold values from -3 to 3
Outputs:
- mean_loss: float32 [], replicated
- watch_grad: float32 [131072, 256], P(('dp', 'tp'))
- search_grad: float32 [131072, 256], P(('dp', 'tp'))
- output_grad: float32 [131072, 256], P(('dp', 'tp'))
- weight_one_grad: float32 [640, 1024], P(None, 'tp')
- bias_one_grad: float32 [1024], P('tp')
- weight_two_grad: float32 [1024, 512], P(None, 'tp')
- bias_two_grad: float32 [512], P('tp')
- weight_three_grad: float32 [512, 256], replicated
- bias_three_grad: float32 [256], replicated
- dense_grad: float32 [4096, 128], P(('dp', 'tp'))
Inputs may be any that keep to these rules, and one draw needn't show every extreme that they name: `watch_ids`: the table has 32 shards; shard s owns rows [s * 4096, (s + 1) * 4096), with 4096 = 4096. Of the 6400 ids in the rows of one index of dp+tp, at most 300 = max(2, 300) lie in one shard, and some shard holds exactly 300 of them. `search_ids`: the table has 32 shards; shard s owns rows [s * 4096, (s + 1) * 4096), with 4096 = 4096. Of the 6400 ids in the rows of one index of dp+tp, at most 300 = max(2, 300) lie in one shard, and some shard holds exactly 300 of them. `positive_ids`: the table has 32 shards; shard s owns rows [s * 4096, (s + 1) * 4096), with 4096 = 4096. Of the 128 ids of one index of dp+tp, at most 6 = max(2, 6) lie in one shard, and some shard holds exactly 6 of them.
All inputs are finite; a program needn't handle non-finite values. No bound on the sum of `search_mask` on one device may be relied on, other than what follows from the above.
Results may differ from a plain program's by a relative error of at most 0.0003.
Values sent between devices are 32-bit elements; how exact they have to be, the bound alone decides.
No kernel may reach another device: no remote copies, remote signals or barrier semaphores. Data moves between devices by JAX's collectives and lax.ppermute only.
A program may use at most 192 MiB of HBM per device.

v0:
```python
import jax
import jax.numpy as jnp
from jax import lax
from jax.sharding import PartitionSpec as P


def matmul(left, right):
    return jnp.dot(left, right, precision=lax.Precision.HIGHEST, preferred_element_type=jnp.float32)


def inner_rows(left, right):
    return lax.dot_general(
        left,
        right,
        (((0,), (0,)), ((), ())),
        precision=lax.Precision.HIGHEST,
        preferred_element_type=jnp.float32,
    )


def buckets(flat_ids, rows_dev, shards, bound):
    count = flat_ids.shape[0]
    owners = flat_ids // rows_dev
    order = jnp.argsort(owners, stable=True)
    sorted_owner = owners[order]
    counts = jnp.sum(
        (owners[:, None] == jnp.arange(shards, dtype=jnp.int32)[None, :]).astype(jnp.int32), axis=0
    )
    starts = jnp.cumsum(counts) - counts
    rank = jnp.arange(count, dtype=jnp.int32) - starts[sorted_owner]
    slots = jnp.zeros((count,), jnp.int32).at[order].set(sorted_owner * bound + rank)
    request = jnp.zeros((shards * bound,), jnp.int32).at[slots].set(flat_ids % rows_dev)
    return (slots, request.reshape(shards, bound))


def softmax_part(user_vec, pos_rows, logq_pos, neg_rows, logq_neg):
    rows, width = user_vec.shape
    block = min(512, rows)
    count = rows // block

    def step(carry, pieces):
        neg_acc, loss_acc = carry
        users_here, pos_here, logq_here = pieces
        s_neg = matmul(users_here, neg_rows.T) - logq_neg[None, :]
        s_pos = jnp.sum(users_here * pos_here, axis=1) - logq_here
        top = jnp.maximum(jnp.max(s_neg, axis=1), s_pos)
        e_neg = jnp.exp(s_neg - top[:, None])
        e_pos = jnp.exp(s_pos - top)
        totals = jnp.sum(e_neg, axis=1) + e_pos
        lse = top + jnp.log(totals)
        p_neg = e_neg / totals[:, None]
        g_score = e_pos / totals - 1.0
        g_user = matmul(p_neg, neg_rows) + g_score[:, None] * pos_here
        g_pos = g_score[:, None] * users_here
        neg_acc = neg_acc + inner_rows(p_neg, users_here)
        loss_acc = loss_acc + jnp.sum(lse - s_pos)
        return ((neg_acc, loss_acc), (g_user, g_pos))

    start = (jnp.zeros(neg_rows.shape, jnp.float32), jnp.zeros((), jnp.float32))
    pieces = (
        user_vec.reshape(count, block, width),
        pos_rows.reshape(count, block, width),
        logq_pos.reshape(count, block),
    )
    (neg_grad, loss_sum), (g_user, g_pos) = lax.scan(step, start, pieces)
    return (g_user.reshape(rows, width), g_pos.reshape(rows, width), neg_grad, loss_sum)


def body(
    watch_ids,
    watch_len,
    search_ids,
    search_len,
    search_mask,
    positive_ids,
    logq_pos,
    negative_ids,
    logq_neg,
    dense_feats,
    watch_table,
    search_table,
    out_table,
    weight_one,
    bias_one,
    weight_two,
    bias_two,
    weight_three,
    bias_three,
):
    shards = lax.axis_size(("dp", "tp"))
    mine = lax.axis_index(("dp", "tp"))
    tp_index = lax.axis_index("tp")
    rows_dev, width = watch_table.shape
    users, bag = watch_ids.shape
    bound_ids = max(2, 3 * users * bag // (2 * shards))
    bound_pos = max(2, 3 * users // (2 * shards))
    watch_slots, watch_req = buckets(watch_ids.reshape(-1), rows_dev, shards, bound_ids)
    search_slots, search_req = buckets(search_ids.reshape(-1), rows_dev, shards, bound_ids)
    pos_slots, pos_req = buckets(positive_ids, rows_dev, shards, bound_pos)
    asked = (
        lax.all_to_all(watch_req, ("dp", "tp"), split_axis=0, concat_axis=0, tiled=True),
        lax.all_to_all(search_req, ("dp", "tp"), split_axis=0, concat_axis=0, tiled=True),
        lax.all_to_all(pos_req, ("dp", "tp"), split_axis=0, concat_axis=0, tiled=True),
    )
    served = (watch_table[asked[0]], search_table[asked[1]], out_table[asked[2]])
    fetched = (
        lax.all_to_all(served[0], ("dp", "tp"), split_axis=0, concat_axis=0, tiled=True),
        lax.all_to_all(served[1], ("dp", "tp"), split_axis=0, concat_axis=0, tiled=True),
        lax.all_to_all(served[2], ("dp", "tp"), split_axis=0, concat_axis=0, tiled=True),
    )
    watch_rows = fetched[0].reshape(-1, width)[watch_slots].reshape(users, bag, width)
    search_rows = fetched[1].reshape(-1, width)[search_slots].reshape(users, bag, width)
    pos_rows = fetched[2].reshape(-1, width)[pos_slots]
    slot_range = jnp.arange(bag)[None, :]
    mask_float = search_mask.astype(jnp.float32)
    watch_weight = (slot_range < watch_len[:, None]).astype(jnp.float32) / watch_len.astype(
        jnp.float32
    )[:, None]
    search_weight = (slot_range < search_len[:, None]).astype(jnp.float32) / search_len.astype(
        jnp.float32
    )[:, None]
    search_weight = search_weight * mask_float[:, None]
    watch_avg = jnp.einsum("ub,ube->ue", watch_weight, watch_rows, precision=lax.Precision.HIGHEST)
    search_avg = jnp.einsum(
        "ub,ube->ue", search_weight, search_rows, precision=lax.Precision.HIGHEST
    )
    feats = jnp.concatenate([watch_avg, search_avg, dense_feats], axis=1)
    neg_owned = (negative_ids // rows_dev == mine).astype(jnp.float32)
    neg_local = negative_ids % rows_dev
    neg_rows = lax.psum(out_table[neg_local] * neg_owned[:, None], ("dp", "tp"))
    all_feats = lax.all_gather(feats, "tp", axis=0, tiled=True)
    hidden_a, gelu_one = jax.vjp(jax.nn.gelu, matmul(all_feats, weight_one) + bias_one)
    full_a = lax.all_gather(hidden_a, "tp", axis=1, tiled=True)
    hidden_b, gelu_two = jax.vjp(jax.nn.gelu, matmul(full_a, weight_two) + bias_two)
    full_b, pos_use, logq_use = (
        lax.all_gather(hidden_b, "tp", axis=1, tiled=True),
        lax.all_gather(pos_rows, "tp", axis=0, tiled=True),
        lax.all_gather(logq_pos, "tp", axis=0, tiled=True),
    )
    user_vec, gelu_three = jax.vjp(jax.nn.gelu, matmul(full_b, weight_three) + bias_three)
    g_user, g_pos, neg_grad, loss_sum = softmax_part(
        user_vec, pos_use, logq_use, neg_rows, logq_neg
    )
    (g_three,) = gelu_three(g_user)
    w_three_grad = inner_rows(full_b, g_three)
    b_three_grad = jnp.sum(g_three, axis=0)
    g_full_b = matmul(g_three, weight_three.T)
    part_width = hidden_b.shape[1]
    g_hidden_b = lax.dynamic_slice_in_dim(g_full_b, tp_index * part_width, part_width, 1)
    g_pos_local = lax.dynamic_slice_in_dim(g_pos, tp_index * users, users, 0)
    (g_two,) = gelu_two(g_hidden_b)
    w_two_grad = inner_rows(full_a, g_two)
    b_two_grad = jnp.sum(g_two, axis=0)
    g_hidden_a = lax.psum_scatter(
        matmul(g_two, weight_two.T), "tp", scatter_dimension=1, tiled=True
    )
    (g_one,) = gelu_one(g_hidden_a)
    w_one_grad = inner_rows(all_feats, g_one)
    b_one_grad = jnp.sum(g_one, axis=0)
    g_feats = lax.psum_scatter(matmul(g_one, weight_one.T), "tp", scatter_dimension=0, tiled=True)
    dense_grad = g_feats[:, 2 * width :]
    g_watch_ids = (watch_weight[:, :, None] * g_feats[:, None, :width]).reshape(-1, width)
    g_search_ids = (search_weight[:, :, None] * g_feats[:, None, width : 2 * width]).reshape(
        -1, width
    )
    watch_buffer = (
        jnp.zeros((shards * bound_ids, width), jnp.float32).at[watch_slots].set(g_watch_ids)
    )
    search_buffer = (
        jnp.zeros((shards * bound_ids, width), jnp.float32).at[search_slots].set(g_search_ids)
    )
    pos_buffer = jnp.zeros((shards * bound_pos, width), jnp.float32).at[pos_slots].set(g_pos_local)
    returned = (
        lax.all_to_all(
            watch_buffer.reshape(shards, bound_ids, width),
            ("dp", "tp"),
            split_axis=0,
            concat_axis=0,
            tiled=True,
        ),
        lax.all_to_all(
            search_buffer.reshape(shards, bound_ids, width),
            ("dp", "tp"),
            split_axis=0,
            concat_axis=0,
            tiled=True,
        ),
        lax.all_to_all(
            pos_buffer.reshape(shards, bound_pos, width),
            ("dp", "tp"),
            split_axis=0,
            concat_axis=0,
            tiled=True,
        ),
    )
    watch_grad = (
        jnp.zeros((rows_dev, width), jnp.float32)
        .at[asked[0].reshape(-1)]
        .add(returned[0].reshape(-1, width))
    )
    search_grad = (
        jnp.zeros((rows_dev, width), jnp.float32)
        .at[asked[1].reshape(-1)]
        .add(returned[1].reshape(-1, width))
    )
    (
        w_one_grad,
        b_one_grad,
        w_two_grad,
        b_two_grad,
        w_three_grad,
        b_three_grad,
        neg_total,
        loss_total,
    ) = lax.psum(
        (
            w_one_grad,
            b_one_grad,
            w_two_grad,
            b_two_grad,
            w_three_grad,
            b_three_grad,
            neg_grad,
            loss_sum,
        ),
        "dp",
    )
    output_grad = (
        jnp.zeros((rows_dev, width), jnp.float32)
        .at[asked[2].reshape(-1)]
        .add(returned[2].reshape(-1, width))
    )
    output_grad = output_grad.at[neg_local].add(neg_total * neg_owned[:, None])
    mean_loss = loss_total / jnp.float32(users * shards)
    return (
        mean_loss,
        watch_grad,
        search_grad,
        output_grad,
        w_one_grad,
        b_one_grad,
        w_two_grad,
        b_two_grad,
        w_three_grad,
        b_three_grad,
        dense_grad,
    )


def solution(mesh):
    in_specs = (
        P(("dp", "tp"), None),
        P(("dp", "tp")),
        P(("dp", "tp"), None),
        P(("dp", "tp")),
        P(("dp", "tp")),
        P(("dp", "tp")),
        P(("dp", "tp")),
        P(),
        P(),
        P(("dp", "tp"), None),
        P(("dp", "tp"), None),
        P(("dp", "tp"), None),
        P(("dp", "tp"), None),
        P(None, "tp"),
        P("tp"),
        P(None, "tp"),
        P("tp"),
        P(),
        P(),
    )
    out_specs = (
        P(),
        P(("dp", "tp"), None),
        P(("dp", "tp"), None),
        P(("dp", "tp"), None),
        P(None, "tp"),
        P("tp"),
        P(None, "tp"),
        P("tp"),
        P(),
        P(),
        P(("dp", "tp"), None),
    )
    return jax.shard_map(body, mesh=mesh, in_specs=in_specs, out_specs=out_specs, check_vma=False)
```

profile of v0, /device:TPU:0, one launch (start us, length us, event | category | flops | bytes accessed | tf_op | source)
XLA Modules:
  0.0 1987.7 jit_solution(15982468501444453280)
XLA Ops:
  11.0 6.7 sort.48
  17.8 33.2 %gather_fusion = s32[6400]{0:T(1024)S(1)} fusion(s32[6400]{0:T(1024)S(1)} %get-tuple-element.120, s32[7168]{0:T(1024)S(1)} %pad_clamp_fusion.5), kind=kCustom, calls=%fused_computation | custom fusion | bytes 76800 | tf_op jit(solution)/shard_map/gather | solution.py:25
  57.7 15.7 fusion.45
  73.4 24.0 %scatter_custom_fusion = s32[6400]{0:T(1024)S(1)} fusion(s32[6400]{0:T(1024)S(1)} %compare_select_fusion.21, s32[6400]{0:T(1024)S(1)} %fusion.45, s32[]{:T(128)} %constant.144.clone.1), kind=kCustom, calls=%fused_computation.217 | custom fusion | bytes 25604 | tf_op jit(solution)/shard_map/scatter | solution.py:31
  97.4 23.9 %scatter_custom_fusion.1 = s32[9600]{0:T(1024)S(1)} fusion(s32[6400]{0:T(1024)S(1)} %compare_select_fusion.20, s32[6400]{0:T(1024)S(1)} %get-tuple-element.119, s32[]{:T(128)} %constant.144.clone.1), kind=kCustom, calls=%fused_computation.207 | custom fusion | bytes 38404 | tf_op jit(solution)/shard_map/scatter | solution.py:32
  122.1 7.5 all-to-all-start
  131.7 6.7 sort.49
  138.5 33.2 %gather_fusion.3 = s32[6400]{0:T(1024)S(1)} fusion(s32[6400]{0:T(1024)S(1)} %get-tuple-element.122, s32[7168]{0:T(1024)S(1)} %pad_clamp_fusion.3), kind=kCustom, calls=%fused_computation.3 | custom fusion | bytes 76800 | tf_op jit(solution)/shard_map/gather | solution.py:25
  178.3 15.7 fusion.44
  194.1 24.0 %scatter_custom_fusion.2 = s32[6400]{0:T(1024)S(1)} fusion(s32[6400]{0:T(1024)S(1)} %compare_select_fusion.19, s32[6400]{0:T(1024)S(1)} %fusion.44, s32[]{:T(128)} %constant.144.clone.1), kind=kCustom, calls=%fused_computation.215 | custom fusion | bytes 25604 | tf_op jit(solution)/shard_map/scatter | solution.py:31
  218.1 23.9 %scatter_custom_fusion.3 = s32[9600]{0:T(1024)S(1)} fusion(s32[6400]{0:T(1024)S(1)} %compare_select_fusion.18, s32[6400]{0:T(1024)S(1)} %get-tuple-element.121, s32[]{:T(128)} %constant.144.clone.1), kind=kCustom, calls=%fused_computation.205 | custom fusion | bytes 38404 | tf_op jit(solution)/shard_map/scatter | solution.py:32
  249.1 25.9 %gather_fusion.1 = f32[9600,256]{1,0:T(8,128)} fusion(f32[4096,256]{1,0:T(8,128)} %param.29, s32[10240]{0:T(1024)S(1)} %pad_clamp_fusion.1), kind=kCustom, calls=%fused_computation.1 | custom fusion | bytes 19699200 | tf_op jit(solution)/shard_map/gather | solution.py:105
  275.0 10.0 reshape.626
  291.2 25.8 %gather_fusion.4 = f32[9600,256]{1,0:T(8,128)} fusion(f32[4096,256]{1,0:T(8,128)} %param.30, s32[10240]{0:T(1024)S(1)} %pad_clamp_fusion), kind=kCustom, calls=%fused_computation.4 | custom fusion | bytes 19699200 | tf_op jit(solution)/shard_map/gather | solution.py:105
  317.0 10.0 reshape.689
  327.0 184.5 %all-to-all-done.1 = f32[32,300,256]{2,1,0:T(8,128)} async-done(((f32[32,300,256]{2,1,0:T(8,128)}), f32[32,300,256]{2,1,0:T(8,128)}, u32[]{:S(2)}, u32[]{:S(2)}) %all-to-all-start.1) | async-done | bytes 9830432 | tf_op jit(solution)/shard_map/all_to_all | solution.py:107
  515.9 9.9 reshape.559
  525.9 19.7 gather_fusion.2
  545.6 7.9 reshape.560
  553.5 182.7 %all-to-all-done.3 = f32[32,300,256]{2,1,0:T(8,128)} async-done(((f32[32,300,256]{2,1,0:T(8,128)}), f32[32,300,256]{2,1,0:T(8,128)}, u32[]{:S(2)}, u32[]{:S(2)}) %all-to-all-start.3) | async-done | bytes 9830432 | tf_op jit(solution)/shard_map/all_to_all | solution.py:108
  736.2 10.0 reshape.564
  746.2 19.8 gather_fusion.5
  766.0 7.9 reshape.565
  784.5 14.2 all-gather.6.cloned.1.call-done
  802.5 22.2 %gather_fusion.6 = f32[5000,256]{1,0:T(8,128)} fusion(f32[4096,256]{1,0:T(8,128)} %param.31, s32[5120]{0:T(1024)S(1)} %pad_clamp_fusion.6), kind=kCustom, calls=%fused_computation.6 | custom fusion | bytes 10260000 | tf_op jit(solution)/shard_map/gather | solution.py:130
  843.4 11.6 all_to_all.66
  866.7 7.8 all-to-all-done.5
  875.3 7.6 all-gather
  886.1 102.4 %all-reduce.5.cloned.1.call-done = f32[5000,256]{1,0:T(8,128)} async-done(((f32[5000,256]{1,0:T(8,128)}), f32[5000,256]{1,0:T(8,128)}) %all-reduce.5.cloned.1.call-update) | async-done | bytes 5120016 | tf_op jit(solution)/shard_map/psum | solution.py:130
  988.5 11.2 subtract_reduce_fusion
  1005.9 18.8 fusion.84
  1029.7 30.8 %reduce-scatter.3.cloned.1.call-done = f32[512,256]{1,0:T(8,128)} async-done(((f32[512,1024]{1,0:T(8,128)}), f32[512,256]{1,0:T(8,128)}) %reduce-scatter.3.cloned.1.call-update) | async-done | bytes 524304 | tf_op jit(solution)/shard_map/reduce_scatter | solution.py:154
  1073.2 18.5 reduce-scatter.5.cloned.1.call-done
  1096.1 8.0 mul.289
  1104.1 52.4 %scatter_custom_fusion.8 = f32[9600,256]{1,0:T(8,128)} fusion(s32[6400]{0:T(1024)} %copy-done.27, f32[6400,256]{1,0:T(8,128)} %mul.289, f32[]{:T(128)} %constant.166.clone.1, f32[6400]{0:T(1024)S(1)} %mul.286), kind=kCustom, calls=%fused_computation.28 | custom fusion | flops 1638400 | bytes 16410112 | tf_op jit(solution)/shard_map/scatter | solution.py:170
  1156.4 10.0 reshape.573
  1175.4 8.0 mul.284
  1183.4 52.5 %scatter_custom_fusion.6 = f32[9600,256]{1,0:T(8,128)} fusion(s32[6400]{0:T(1024)} %copy-done.26, f32[6400,256]{1,0:T(8,128)} %mul.284, f32[]{:T(128)} %constant.166.clone.1, f32[6400]{0:T(1024)S(1)} %div.113), kind=kCustom, calls=%fused_computation.30 | custom fusion | flops 1638400 | bytes 16410112 | tf_op jit(solution)/shard_map/scatter | solution.py:167
  1235.9 9.9 reshape.570
  1245.8 146.7 %all-to-all-done.7 = f32[32,300,256]{2,1,0:T(8,128)} async-done(((f32[32,300,256]{2,1,0:T(8,128)}), f32[32,300,256]{2,1,0:T(8,128)}, u32[]{:S(2)}, u32[]{:S(2)}) %all-to-all-start.7) | async-done | bytes 9830432 | tf_op jit(solution)/shard_map/all_to_all | solution.py:181
  1404.6 13.9 fusion.70
  1427.8 227.6 %all-reduce = (f32[]{:T(128)}, f32[256]{0:T(256)}, f32[128]{0:T(128)}, f32[256]{0:T(256)}) all-reduce(f32[]{:T(128)} %get-tuple-element.124, f32[256]{0:T(256)S(1)} %copy-done.33, f32[128]{0:T(128)S(1)} %copy-done.34, f32[256]{0:T(256)S(1)} %copy-done.39), channel_id=1, replica_groups=mesh['dp'=8,'tp'=4] {'dp'}, use_global_device_ids=true, to_apply=%region_20.21 | all-reduce | flops 641 | bytes 5128 | tf_op jit(solution)/shard_map/psum | solution.py:215
  1657.5 143.5 %all-reduce.7.cloned.1.call-done = (f32[5000,256]{1,0:T(8,128)}, f32[640,256]{1,0:T(8,128)}, f32[1024,128]{1,0:T(8,128)}, f32[512,256]{1,0:T(8,128)}) async-done(((f32[5000,256]{1,0:T(8,128)}, f32[640,256]{1,0:T(8,128)}, f32[1024,128]{1,0:T(8,128)}, f32[512,256]{1,0:T(8,128)}), (f32[5000,256]{1,0:T(8,128)}, f32[640,256]{1,0:T(8,128)}, f32[1024,128]{1,0:T(8,128)}, ...) | async-done | bytes 6823952 | tf_op jit(solution)/shard_map/psum | solution.py:215
  1801.0 43.5 %scatter_custom_fusion.12 = f32[4096,256]{1,0:T(8,128)} fusion(f32[4096,256]{1,0:T(8,128)} %scatter_custom_fusion.11, s32[5000]{0:T(1024)} %copy-done.29, f32[5000,256]{1,0:T(8,128)} %get-tuple-element.101, f32[5000]{0:T(1024)S(1)} %copy-done.25), kind=kCustom, calls=%fused_computation.32 | custom fusion | flops 2560000 | bytes 9334304 | tf_op jit(solution)/shard_map/scatter-add | solution.py:233
  1844.5 9.9 reshape.820
  1854.4 56.1 %scatter_custom_fusion.9 = f32[4096,256]{1,0:T(8,128)} fusion(s32[9600]{0:T(1024)S(1)} %fusion.43, f32[9600,256]{1,0:T(8,128)} %reshape.820, f32[]{:T(128)} %constant.166.clone.1), kind=kCustom, calls=%fused_computation.42 | custom fusion | flops 2457600 | bytes 4194816 | tf_op jit(solution)/shard_map/scatter-add | solution.py:204
  1910.5 10.0 reshape.804
  1920.5 56.3 %scatter_custom_fusion.7 = f32[4096,256]{1,0:T(8,128)} fusion(s32[9600]{0:T(1024)S(1)} %fusion.42, f32[9600,256]{1,0:T(8,128)} %reshape.804, f32[]{:T(128)} %constant.166.clone.1), kind=kCustom, calls=%fused_computation.44 | custom fusion | flops 2457600 | bytes 4194816 | tf_op jit(solution)/shard_map/scatter-add | solution.py:199
  (247 shorter events, 147.5 us)
Async XLA Ops:
  8.0 790.7 %copy-start = (f32[640,256]{1,0:T(8,128)S(1)}, f32[640,256]{1,0:T(8,128)}, u32[]{:S(2)}) copy-start(f32[640,256]{1,0:T(8,128)} %param.32) | copy-start | bytes 1966084
  17.7 111.8 %copy-start.31 = (s32[128,50]{0,1:T(8,128)S(1)}, s32[128,50]{0,1:T(8,128)}, u32[]{:S(2)}) copy-start(s32[128,50]{0,1:T(8,128)} %param.21) | copy-start | bytes 76804
  97.4 418.3 %copy-start.26 = (s32[6400]{0:T(1024)}, s32[6400]{0:T(1024)S(1)}, u32[]{:S(2)}) copy-start(s32[6400]{0:T(1024)S(1)} %compare_select_fusion.20) | copy-start | bytes 76804
  122.1 120.7 %all-to-all-start = ((s32[32,1,300]{2,1,0:T(1,128)}), s32[32,1,300]{2,1,0:T(1,128)S(1)}, u32[]{:S(2)}, u32[]{:S(2)}) async-start(s32[32,1,300]{2,1,0:T(1,128)} %all_to_all.42), calls=%async_computation | async-start | bytes 98304 | tf_op jit(solution)/shard_map/all_to_all | solution.py:101
  218.0 297.6 %copy-start.27 = (s32[6400]{0:T(1024)}, s32[6400]{0:T(1024)S(1)}, u32[]{:S(2)}) copy-start(s32[6400]{0:T(1024)S(1)} %compare_select_fusion.18) | copy-start | bytes 76804
  242.8 32.2 %copy-start.20 = (s32[32,1,300]{2,1,0:T(1,128)}, s32[32,1,300]{2,1,0:T(1,128)S(1)}, u32[]{:S(2)}) copy-start(s32[32,1,300]{2,1,0:T(1,128)S(1)} %all-to-all-done) | copy-start | bytes 115204
  242.8 42.1 %all-to-all-start.2 = ((s32[32,1,300]{2,1,0:T(1,128)}), s32[32,1,300]{2,1,0:T(1,128)S(1)}, u32[]{:S(2)}, u32[]{:S(2)}) async-start(s32[32,1,300]{2,1,0:T(1,128)} %all_to_all.46), calls=%async_computation.2 | async-start | bytes 98304 | tf_op jit(solution)/shard_map/all_to_all | solution.py:102
  284.9 226.6 %all-to-all-start.1 = ((f32[32,300,256]{2,1,0:T(8,128)}), f32[32,300,256]{2,1,0:T(8,128)}, u32[]{:S(2)}, u32[]{:S(2)}) async-start(f32[32,300,256]{2,1,0:T(8,128)} %reshape.626), calls=%async_computation.1 | async-start | bytes 19922944 | tf_op jit(solution)/shard_map/all_to_all | solution.py:107
  327.0 188.5 %copy-start.45 = (s32[128]{0:T(128)S(1)}, s32[128]{0:T(128)}, u32[]{:S(2)}) copy-start(s32[128]{0:T(128)} %param.23) | copy-start | bytes 1540
  327.0 188.5 %copy-start.40 = (s32[128]{0:T(128)S(1)}, s32[128]{0:T(128)}, u32[]{:S(2)}) copy-start(s32[128]{0:T(128)} %param.20) | copy-start | bytes 1540
  327.0 188.6 %copy-start.41 = (s32[128]{0:T(128)S(1)}, s32[128]{0:T(128)}, u32[]{:S(2)}) copy-start(s32[128]{0:T(128)} %param.22) | copy-start | bytes 1540
  511.6 224.6 %all-to-all-start.3 = ((f32[32,300,256]{2,1,0:T(8,128)}), f32[32,300,256]{2,1,0:T(8,128)}, u32[]{:S(2)}, u32[]{:S(2)}) async-start(f32[32,300,256]{2,1,0:T(8,128)} %reshape.689), calls=%async_computation.3 | async-start | bytes 19922944 | tf_op jit(solution)/shard_map/all_to_all | solution.py:108
  515.3 283.4 %all-gather.6.cloned.1.call-start = ((), (), s32[]{:S(2)}) async-start(), calls=%async_computation.11 | async-start | bytes 1638400 | tf_op jit(solution)/shard_map/all_gather | solution.py:131
  515.8 258.1 %copy-start.13 = (f32[128,50]{1,0:T(8,128)}, f32[128,50]{1,0:T(8,128)S(1)}, u32[]{:S(2)}) copy-start(f32[128,50]{1,0:T(8,128)S(1)} %convert_divide_fusion) | copy-start | bytes 76804
  515.9 264.0 %copy-start.15 = (f32[128,50]{1,0:T(8,128)}, f32[128,50]{1,0:T(8,128)S(1)}, u32[]{:S(2)}) copy-start(f32[128,50]{1,0:T(8,128)S(1)} %divide_multiply_fusion) | copy-start | bytes 76804
  773.9 24.8 %copy-start.38 = (f32[256]{0:T(256)S(1)}, f32[256]{0:T(256)}, u32[]{:S(2)}) copy-start(f32[256]{0:T(256)} %param.33) | copy-start | bytes 3076
  779.9 22.5 %copy-start.28 = (s32[5000]{0:T(1024)S(1)}, s32[5000]{0:T(1024)}, u32[]{:S(2)}) copy-start(s32[5000]{0:T(1024)} %param.26) | copy-start | bytes 60004
  784.5 40.6 %all-gather.8.cloned.1.call-start = ((), (), s32[]{:S(2)}) async-start(), calls=%async_computation.12 | async-start | bytes 2621440 | tf_op jit(solution)/shard_map/all_gather | solution.py:133
  802.4 80.5 %all-gather.10.cloned.1.call-start = ((), (), s32[]{:S(2)}) async-start(), calls=%async_computation.13 | async-start | bytes 1310720 | tf_op jit(solution)/shard_map/all_gather | solution.py:136
  802.5 22.3 %copy-start.29 = (s32[5000]{0:T(1024)}, s32[5000]{0:T(1024)S(1)}, u32[]{:S(2)}) copy-start(s32[5000]{0:T(1024)S(1)} %compare_select_fusion.22) | copy-start | bytes 60004
  802.5 22.6 %copy-start.6 = (f32[1024,128]{1,0:T(8,128)S(1)}, f32[1024,128]{1,0:T(8,128)}, u32[]{:S(2)}) copy-start(f32[1024,128]{1,0:T(8,128)} %param.34) | copy-start | bytes 1572868
  802.5 22.6 %copy-start.44 = (f32[128]{0:T(128)S(1)}, f32[128]{0:T(128)}, u32[]{:S(2)}) copy-start(f32[128]{0:T(128)} %param.35) | copy-start | bytes 1540
  829.4 159.1 %all-reduce.5.cloned.1.call-start = ((), (), s32[]{:S(2)}) async-start(), calls=%async_computation.14 | async-start | bytes 10240000 | tf_op jit(solution)/shard_map/psum | solution.py:130
  835.8 25.9 %copy-start.42 = (f32[128]{0:T(128)S(1)}, f32[128]{0:T(128)}, u32[]{:S(2)}) copy-start(f32[128]{0:T(128)} %param.25) | copy-start | bytes 1540
  835.8 47.1 %copy-start.5 = (f32[512,256]{1,0:T(8,128)S(1)}, f32[512,256]{1,0:T(8,128)}, u32[]{:S(2)}) copy-start(f32[512,256]{1,0:T(8,128)} %param.36) | copy-start | bytes 1572868
  835.8 47.1 %copy-start.37 = (f32[256]{0:T(256)S(1)}, f32[256]{0:T(256)}, u32[]{:S(2)}) copy-start(f32[256]{0:T(256)} %param.37) | copy-start | bytes 3076
  835.8 152.7 %copy-start.19 = (f32[5000]{0:T(1024)S(1)}, f32[5000]{0:T(1024)}, u32[]{:S(2)}) copy-start(f32[5000]{0:T(1024)} %param.27) | copy-start | bytes 60004
  842.3 32.2 %copy-start.43 = (s32[128]{0:T(128)}, s32[128]{0:T(128)S(1)}, u32[]{:S(2)}) copy-start(s32[128]{0:T(128)S(1)} %compare_select_fusion.25) | copy-start | bytes 1540
  859.0 15.5 all-to-all-start.5
  861.6 198.9 %reduce-scatter.3.cloned.1.call-start = ((), (), s32[]{:S(2)}) async-start(), calls=%async_computation.15 | async-start | bytes 2621440 | tf_op jit(solution)/shard_map/reduce_scatter | solution.py:154
  886.1 116.9 %copy-start.8 = (f32[512,256]{1,0:T(8,128)}, f32[512,256]{1,0:T(8,128)S(1)}, u32[]{:S(2)}) copy-start(f32[512,256]{1,0:T(8,128)S(1)} %get-tuple-element.198) | copy-start | bytes 1572868
  999.7 25.0 %copy-start.1 = (f32[512,5000]{0,1:T(8,128)}, f32[512,5000]{0,1:T(8,128)S(1)}, u32[]{:S(2)}) copy-start(f32[512,5000]{0,1:T(8,128)S(1)} %get-tuple-element.197) | copy-start | bytes 30720004
  999.7 25.0 %copy-start.32 = (f32[512]{0:T(512)}, f32[512]{0:T(512)S(1)}, u32[]{:S(2)}) copy-start(f32[512]{0:T(512)S(1)} %get-tuple-element.109) | copy-start | bytes 6148
  1003.0 21.7 %copy-start.35 = (f32[512]{0:T(512)}, f32[512]{0:T(512)S(1)}, u32[]{:S(2)}) copy-start(f32[512]{0:T(512)S(1)} %get-tuple-element.123) | copy-start | bytes 6148
  1003.0 21.7 %copy-start.36 = (f32[512]{0:T(512)}, f32[512]{0:T(512)S(1)}, u32[]{:S(2)}) copy-start(f32[512]{0:T(512)S(1)} %get-tuple-element.125) | copy-start | bytes 6148
  1005.9 19.9 %copy-start.11 = (f32[512,128]{1,0:T(8,128)S(1)}, f32[512,128]{1,0:T(8,128)}, u32[]{:S(2)}) copy-start(f32[512,128]{1,0:T(8,128)} %get-tuple-element.195) | copy-start | bytes 786436
  1025.8 47.3 %copy-start.16 = (f32[128,50]{1,0:T(8,128)S(1)}, f32[128,50]{1,0:T(8,128)}, u32[]{:S(2)}) copy-start(f32[128,50]{1,0:T(8,128)} %copy-done.15) | copy-start | bytes 76804
  1029.7 62.0 %reduce-scatter.5.cloned.1.call-start = ((), (), s32[]{:S(2)}) async-start(), calls=%async_computation.16 | async-start | bytes 1638400 | tf_op jit(solution)/shard_map/reduce_scatter | solution.py:160
  1068.0 98.4 %all-to-all-start.8 = ((f32[32,6,256]{2,1,0:T(8,128)}), f32[32,6,256]{2,1,0:T(8,128)S(1)}, u32[]{:S(2)}, u32[]{:S(2)}) async-start(f32[32,6,256]{2,1,0:T(8,128)} %reshape.576), calls=%async_computation.10 | async-start | bytes 524288 | tf_op jit(solution)/shard_map/all_to_all | solution.py:188
  1167.1 225.4 %all-to-all-start.7 = ((f32[32,300,256]{2,1,0:T(8,128)}), f32[32,300,256]{2,1,0:T(8,128)}, u32[]{:S(2)}, u32[]{:S(2)}) async-start(f32[32,300,256]{2,1,0:T(8,128)} %reshape.573), calls=%async_computation.9 | async-start | bytes 19922944 | tf_op jit(solution)/shard_map/all_to_all | solution.py:181
  1245.8 154.6 %copy-start.3 = (f32[512,1024]{1,0:T(8,128)S(1)}, f32[512,1024]{1,0:T(8,128)}, u32[]{:S(2)}) copy-start(f32[512,1024]{1,0:T(8,128)} %all-gather.8.cloned.1.call-done) | copy-start | bytes 6291460
  1392.5 518.0 %all-to-all-start.6 = ((f32[32,300,256]{2,1,0:T(8,128)}), f32[32,300,256]{2,1,0:T(8,128)}, u32[]{:S(2)}, u32[]{:S(2)}) async-start(f32[32,300,256]{2,1,0:T(8,128)} %reshape.570), calls=%async_computation.8 | async-start | bytes 19922944 | tf_op jit(solution)/shard_map/all_to_all | solution.py:174
  1396.2 404.8 %all-reduce.7.cloned.1.call-start = ((), (), s32[]{:S(2)}) async-start(), calls=%async_computation.17 | async-start | bytes 13647872 | tf_op jit(solution)/shard_map/psum | solution.py:215
  1404.6 13.9 copy-start.4
  1421.7 379.3 %copy-start.25 = (f32[5000]{0:T(1024)S(1)}, f32[5000]{0:T(1024)}, u32[]{:S(2)}) copy-start(f32[5000]{0:T(1024)} %copy-done.24) | copy-start | bytes 60004
  1910.5 66.3 %copy-start.12 = (f32[640,256]{1,0:T(8,128)S(1)}, f32[640,256]{1,0:T(8,128)}, u32[]{:S(2)}) copy-start(f32[640,256]{1,0:T(8,128)} %get-tuple-element.207) | copy-start | bytes 1966084
  1910.5 67.1 %copy-start.18 = (f32[1024,128]{1,0:T(8,128)S(1)}, f32[1024,128]{1,0:T(8,128)}, u32[]{:S(2)}) copy-start(f32[1024,128]{1,0:T(8,128)} %get-tuple-element.209) | copy-start | bytes 1572868
  1920.5 57.9 %copy-start.17 = (f32[512,256]{1,0:T(8,128)S(1)}, f32[512,256]{1,0:T(8,128)}, u32[]{:S(2)}) copy-start(f32[512,256]{1,0:T(8,128)} %get-tuple-element.211) | copy-start | bytes 1572868
  (16 other events, 79.3 us)
Sparse Core Ops, SparseCore 0:
  784.6 14.0 all-gather.5
  802.5 22.5 all-gather.7
  829.5 17.0 all-gather.9
  1029.8 30.6 reduce-scatter.2
  1065.1 26.5 reduce-scatter.4
Sparse Core Ops, SparseCore 1:
  835.9 152.5 all-reduce.4
  1421.8 379.2 all-reduce.6
where the time goes:
time: 2000 us; the launch traced here: 1990 us
  waiting for transfers between devices  832 us (42%)
  local copies, waits for them, and re-layouts  422 us (21%)
  other arithmetic  342 us (17%)
  blocking collectives  252 us (13%)
  matrix products  82.6 us (4%)
  starting transfers between devices  40.2 us (2%)
    psum x1, blocking collectives, body(): lax.psum((w_one_grad, b_one_grad, w_two_grad, b_two_grad, w_three_grad, b...  228 us
    all_to_all x1, waiting for transfers between devices, body(): lax.all_to_all(served[0], ('dp', 'tp'), split_axis=0, concat_axis=0, tile...  185 us
    all_to_all x1, waiting for transfers between devices, body(): lax.all_to_all(served[1], ('dp', 'tp'), split_axis=0, concat_axis=0, tile...  183 us
    all_to_all x1, waiting for transfers between devices, body(): lax.all_to_all(search_buffer.reshape(shards, bound_ids, width), ('dp', 't...  147 us
    psum x1, waiting for transfers between devices, body(): lax.psum((w_one_grad, b_one_grad, w_two_grad, b_two_grad, w_three_grad, b...  144 us
    psum x1, waiting for transfers between devices, body(): neg_rows = lax.psum(out_table[neg_local] * neg_owned[:, None], ('dp', 'tp'))  102 us
    gather x3, local copies, waits for them, and re-layouts, buckets(): sorted_owner = owners[order]  67.7 us
    scatter-add x1, other arithmetic, body(): watch_grad = jnp.zeros((rows_dev, width), jnp.float32).at[asked[0].reshap...  56.3 us
  transfers between devices with their start and end apart: 15, of which 10 were waited for; matrix products, arithmetic and copies ran while one was open for 28% of the time, Pallas kernels for 0%

commit v1 on v0

v1 whole, which is shorter than its diff:
```python
import functools

import jax
import jax.numpy as jnp
from jax import lax
from jax.experimental import pallas as pl
from jax.experimental.pallas import tpu as pltpu
from jax.sharding import PartitionSpec as P

AXES = ("dp", "tp")
F32 = jnp.float32
I32 = jnp.int32
BIG = 1e30
LANES = 128
GROUP = 4
UNROLL = 4
SHIFT = 8
PAD_ROWS = 8


def matmul(left, right):
    return jnp.dot(left, right, precision=lax.Precision.HIGH, preferred_element_type=F32)


def matmul_t(left, right):
    return lax.dot_general(
        left, right, (((1,), (1,)), ((), ())), precision=lax.Precision.HIGH, preferred_element_type=F32
    )


def inner_rows(left, right):
    return lax.dot_general(
        left, right, (((0,), (0,)), ((), ())), precision=lax.Precision.HIGH, preferred_element_type=F32
    )


def swap(x, mask, shards):
    return lax.ppermute(x, AXES, [(i, i ^ mask) for i in range(shards)])


def places(order):
    n = len(order)
    return [sum(((p >> (n - 1 - j)) & 1) << order[j] for j in range(n)) for p in range(1 << n)]


def group_max(cnt_ref, group):
    most = cnt_ref[group * GROUP]
    for k in range(1, GROUP):
        most = jnp.maximum(most, cnt_ref[group * GROUP + k])
    return (most + UNROLL - 1) // UNROLL


def load_indices(idx_ref, group, step, cap):
    base = (group * cap + step * UNROLL) * GROUP
    return [[idx_ref[base + u * GROUP + k] for k in range(GROUP)] for u in range(UNROLL)]


def pool_kernel(groups, users, cap, cnt_ref, idx_ref, tab_ref, send_ref, keep_ref, tab):
    rows = tab_ref.shape[0]
    for h in range(2):
        tab[pl.ds(h, rows, 2), :] = tab_ref[:, h * LANES : (h + 1) * LANES]
    tab[pl.ds(2 * rows, 2 * PAD_ROWS), :] = jnp.zeros((2 * PAD_ROWS, LANES), F32)
    send_ref[...] = jnp.zeros_like(send_ref)
    keep_ref[...] = jnp.zeros_like(keep_ref)
    half = len(groups) // 2
    for place, group in enumerate(groups):
        out = keep_ref if place < half else send_ref
        first = (place % half) * GROUP * users

        def step(i, carry, out=out, first=first, group=group):
            picks = load_indices(idx_ref, group, i, cap)
            source = [[tab[pl.ds(pl.multiple_of((v >> SHIFT) * 2, 2), 2), :] for v in row] for row in picks]
            for u in range(UNROLL):
                where = [first + k * users + (v & ((1 << SHIFT) - 1)) for k, v in enumerate(picks[u])]
                held = [out[w] for w in where]
                for k in range(GROUP):
                    out[where[k]] = held[k] + source[u][k]
            return carry

        lax.fori_loop(0, group_max(cnt_ref, group), step, 0)


def pool(groups, users, cap, counts, index, table):
    rows, width = table.shape
    shards = len(groups) * GROUP
    return pl.pallas_call(
        functools.partial(pool_kernel, groups, users, cap),
        out_shape=[jax.ShapeDtypeStruct((shards // 2 * users, 2, LANES), F32)] * 2,
        in_specs=[pl.BlockSpec(memory_space=pltpu.SMEM)] * 2 + [pl.BlockSpec(memory_space=pltpu.VMEM)],
        out_specs=[pl.BlockSpec(memory_space=pltpu.VMEM)] * 2,
        scratch_shapes=[pltpu.VMEM((2 * (rows + PAD_ROWS), LANES), F32)],
        compiler_params=pltpu.CompilerParams(vmem_limit_bytes=60 << 20),
        cost_estimate=pl.CostEstimate(flops=0, bytes_accessed=40 << 20, transcendentals=0),
    )(counts, index, table)


def spread_kernel(groups, users, cap, cnt_ref, idx_ref, near_ref, far_ref, out_ref, acc):
    rows = out_ref.shape[0]
    acc[...] = jnp.zeros_like(acc)
    half = len(groups) // 2
    for place, group in enumerate(groups):
        source_ref = near_ref if place < half else far_ref
        first = (place % half) * GROUP * users

        def step(i, carry, source_ref=source_ref, first=first, group=group):
            picks = load_indices(idx_ref, group, i, cap)
            source = [
                [source_ref[first + k * users + (v & ((1 << SHIFT) - 1))] for k, v in enumerate(row)]
                for row in picks
            ]
            for u in range(UNROLL):
                for k in range(GROUP):
                    where = pl.ds(pl.multiple_of((picks[u][k] >> SHIFT) * 2, 2), 2)
                    acc[where, :] = acc[where, :] + source[u][k]
            return carry

        lax.fori_loop(0, group_max(cnt_ref, group), step, 0)
    for h in range(2):
        out_ref[:, h * LANES : (h + 1) * LANES] = acc[pl.ds(h, rows, 2), :]


def spread(groups, users, cap, rows, counts, index, near, far):
    width = near.shape[1] * near.shape[2]
    return pl.pallas_call(
        functools.partial(spread_kernel, groups, users, cap),
        out_shape=jax.ShapeDtypeStruct((rows, width), F32),
        in_specs=[pl.BlockSpec(memory_space=pltpu.SMEM)] * 2 + [pl.BlockSpec(memory_space=pltpu.VMEM)] * 2,
        out_specs=pl.BlockSpec(memory_space=pltpu.VMEM),
        scratch_shapes=[pltpu.VMEM((2 * (rows + PAD_ROWS), LANES), F32)],
        compiler_params=pltpu.CompilerParams(vmem_limit_bytes=60 << 20),
        cost_estimate=pl.CostEstimate(flops=0, bytes_accessed=40 << 20, transcendentals=0),
    )(counts, index, near, far)


def shard_counts(owners, shards):
    return jnp.sum((owners[:, None] == jnp.arange(shards, dtype=I32)[None, :]).astype(I32), axis=0)


def fill_owners(owners, shards, cap):
    lack = cap - shard_counts(owners, shards)
    ends = jnp.sum(jnp.tril(jnp.ones((shards, shards), I32)) * lack[None, :], axis=1)
    extra = jnp.arange(shards * cap - owners.shape[0], dtype=I32)
    return jnp.sum((extra[:, None] >= ends[None, :]).astype(I32), axis=1)


def request_keys(table, ids, used, user, users, rows, shards, cap):
    owner = ids // rows
    unit = rows * users
    real = ((table * shards + owner) * 2 + (1 - used)) * unit + (ids % rows) * users + user
    extra = ((table * shards + fill_owners(owner, shards, cap)) * 2 + 1) * unit
    return [real, extra]


def decode_keys(keys, users, rows):
    used = (keys // (rows * users)) % 2 == 0
    return jnp.where(used, (keys // users) % rows, rows), jnp.where(used, keys % users, 0)


def body(
    watch_ids,
    watch_len,
    search_ids,
    search_len,
    search_mask,
    positive_ids,
    logq_pos,
    negative_ids,
    logq_neg,
    dense_feats,
    watch_table,
    search_table,
    out_table,
    weight_one,
    bias_one,
    weight_two,
    bias_two,
    weight_three,
    bias_three,
):
    shards = lax.axis_size(AXES)
    n_tp = lax.axis_size("tp")
    n_dp = shards // n_tp
    mine = lax.axis_index(AXES)
    tp = lax.axis_index("tp")
    dp = lax.axis_index("dp")
    bits = shards.bit_length() - 1
    tp_bits = n_tp.bit_length() - 1
    rows, width = watch_table.shape
    users, bag = watch_ids.shape
    negs = negative_ids.shape[0]
    cap = max(2, 3 * users * bag // (2 * shards))
    cap_pos = max(2, 3 * users // (2 * shards))
    cap_pad = -(-cap // UNROLL) * UNROLL
    order_a = list(range(bits))
    order_b = [0, 2, 1] + list(range(3, bits))
    place_a, place_b = places(order_a), places(order_b)
    groups_a = list(range(shards // GROUP))
    groups_b = [place_a.index(place_b[g * GROUP]) // GROUP for g in groups_a]

    mean = negs / shards
    block = min(-(-negs // 8) * 8, max(8, int(mean + 4.2 * mean**0.5) // 8 * 8))
    neg_owner = negative_ids // rows
    neg_count = shard_counts(neg_owner, shards)
    neg_most = jnp.max(neg_count)
    neg_mine = neg_owner == mine
    own_rows_id, own_logq = lax.sort(
        (jnp.where(neg_mine, negative_ids % rows, rows), logq_neg), num_keys=1
    )
    own_rows_id = jnp.concatenate([own_rows_id, jnp.full((block,), rows, I32)])
    own_logq = jnp.concatenate([own_logq, jnp.full((block,), BIG, F32)])
    first_id = own_rows_id[:block]
    first_logq = jnp.where(first_id < rows, own_logq[:block], 0.0)
    logq_rows = -(-block // (8 * width)) * 8
    own_rows = out_table[jnp.minimum(first_id, rows - 1)]
    payload = jnp.concatenate(
        [own_rows, jnp.pad(first_logq, (0, logq_rows * width - block)).reshape(logq_rows, width)]
    )
    gathered = lax.all_gather(payload, AXES, axis=0, tiled=False)
    neg_rows = gathered.reshape(-1, width)
    neg_real = jnp.arange(block, dtype=I32)[None, :] < neg_count[:, None]
    neg_logq = jnp.where(neg_real, gathered[:, block:, :].reshape(shards, -1)[:, :block], BIG)
    neg_logq = jnp.pad(neg_logq, ((0, 0), (0, logq_rows)), constant_values=BIG).reshape(-1)
    n_all = neg_rows.shape[0]

    w_one = lax.all_gather(weight_one, "tp", axis=1, tiled=True)
    w_two = lax.all_gather(weight_two, "tp", axis=1, tiled=True)
    b_one = lax.all_gather(bias_one, "tp", axis=0, tiled=True)
    b_two = lax.all_gather(bias_two, "tp", axis=0, tiled=True)

    slot = jnp.arange(users * bag, dtype=I32)
    slot_user = slot // bag
    spot = jnp.arange(bag, dtype=I32)[None, :]
    watch_used = (spot < watch_len[:, None]).astype(I32).reshape(-1)
    search_used = ((spot < search_len[:, None]) & (search_mask[:, None] > 0)).astype(I32).reshape(-1)
    user_index = jnp.arange(users, dtype=I32)
    keys = jnp.concatenate(
        request_keys(0, watch_ids.reshape(-1), watch_used, slot_user, users, rows, shards, cap)
        + request_keys(1, search_ids.reshape(-1), search_used, slot_user, users, rows, shards, cap)
        + request_keys(2, positive_ids, 1, user_index, users, rows, shards, cap_pos)
    )
    keys = lax.sort(keys)
    parts = [
        keys[: shards * cap].reshape(shards, cap),
        keys[shards * cap : 2 * shards * cap].reshape(shards, cap),
        keys[2 * shards * cap :].reshape(shards, cap_pos),
    ]
    decoded = [piece for part in parts for piece in decode_keys(part, users, rows)]
    request = jnp.concatenate(decoded, axis=1)
    my_pos_user = jnp.where(decoded[4] < rows, decoded[5], -1)
    asked = lax.all_to_all(
        request.reshape(shards, 1, -1), AXES, split_axis=0, concat_axis=0, tiled=True
    ).reshape(shards, -1)
    pos_row = asked[:, 4 * cap : 4 * cap + cap_pos]
    pos_user = asked[:, 4 * cap + cap_pos :]
    near_first = asked[mine ^ jnp.array(place_a, I32), : 4 * cap]

    def prepared(start):
        row = near_first[:, start : start + cap]
        user = near_first[:, start + cap : start + 2 * cap]
        counts = jnp.sum((row < rows).astype(I32), axis=1)
        packed = jnp.pad(row * (1 << SHIFT) + user, ((0, 0), (0, cap_pad - cap)), constant_values=rows << SHIFT)
        packed = packed.reshape(shards // GROUP, GROUP, cap_pad).transpose(0, 2, 1).reshape(-1)
        return counts, packed

    watch_plan, search_plan = prepared(0), prepared(2 * cap)

    def scatter_sum(order, send, keep):
        total = keep + swap(send, 1 << order[0], shards)
        for b in order[1:]:
            half = total.shape[0] // 2
            total = total[:half] + swap(total[half:], 1 << b, shards)
        return total.reshape(users, width)

    watch_send, watch_keep = pool(groups_a, users, cap_pad, *watch_plan, watch_table)
    search_send, search_keep = pool(groups_b, users, cap_pad, *search_plan, search_table)
    watch_sum = scatter_sum(order_a, watch_send, watch_keep)
    search_sum = scatter_sum(order_b, search_send, search_keep)
    watch_scale = 1.0 / watch_len.astype(F32)[:, None]
    search_scale = search_mask.astype(F32)[:, None] / search_len.astype(F32)[:, None]
    feats = jnp.concatenate([watch_sum * watch_scale, search_sum * search_scale, dense_feats], axis=1)

    served = out_table[jnp.minimum(pos_row, rows - 1)]
    fetched = lax.all_to_all(served, AXES, split_axis=0, concat_axis=0, tiled=True).reshape(-1, width)
    pos_match = my_pos_user.reshape(-1)[None, :] == user_index[:, None]
    pos_slot = jnp.sum(
        jnp.where(pos_match, jnp.arange(shards * cap_pos, dtype=I32)[None, :], 0), axis=1
    )
    pos_rows = fetched[pos_slot]

    def all_negatives(state):
        local = jnp.where(neg_mine[:, None], out_table[negative_ids % rows], 0.0)
        full = lax.psum(local, AXES)
        return (
            jnp.zeros((), I32),
            jnp.pad(full, ((0, max(0, n_all - negs)), (0, 0)))[:n_all],
            jnp.pad(logq_neg, (0, max(0, n_all - negs)), constant_values=BIG)[:n_all],
        )

    overflow = (neg_most > block).astype(I32)
    _, neg_rows, neg_logq = lax.while_loop(
        lambda state: state[0] > 0, all_negatives, (overflow, neg_rows, neg_logq)
    )

    hidden_a, gelu_one = jax.vjp(jax.nn.gelu, matmul(feats, w_one) + b_one)
    hidden_b, gelu_two = jax.vjp(jax.nn.gelu, matmul(hidden_a, w_two) + b_two)
    user_vec, gelu_three = jax.vjp(jax.nn.gelu, matmul(hidden_b, weight_three) + bias_three)

    user_all = lax.all_gather(user_vec, AXES, axis=0, tiled=True)
    s_neg = matmul_t(user_vec, neg_rows) - neg_logq[None, :]
    s_pos = jnp.sum(user_vec * pos_rows, axis=1) - logq_pos
    top = jnp.maximum(jnp.max(s_neg, axis=1), s_pos)
    e_neg = jnp.exp(s_neg - top[:, None])
    e_pos = jnp.exp(s_pos - top)
    totals = jnp.sum(e_neg, axis=1) + e_pos
    lse = top + jnp.log(totals)
    coef = e_pos / totals - 1.0
    g_user = matmul(e_neg, neg_rows) / totals[:, None] + coef[:, None] * pos_rows
    loss_sum = jnp.sum(lse - s_pos)
    stats = lax.all_gather(jnp.stack([lse, coef]), AXES, axis=0, tiled=False)
    lse_all = stats[:, 0].reshape(-1)
    coef_all = stats[:, 1].reshape(-1)

    (g_three,) = gelu_three(g_user)
    (g_two,) = gelu_two(matmul_t(g_three, weight_three))
    (g_one,) = gelu_one(matmul_t(g_two, w_two))
    g_feats = matmul_t(g_one, w_one)
    dense_grad = g_feats[:, 2 * width :]

    def gather_all(order, x):
        x = x.reshape(users, 2, LANES)
        for b in reversed(order[1:]):
            x = jnp.concatenate([x, swap(x, 1 << b, shards)])
        return x, swap(x, 1 << order[0], shards)

    watch_near, watch_far = gather_all(order_a, g_feats[:, :width] * watch_scale)
    search_near, search_far = gather_all(order_b, g_feats[:, width : 2 * width] * search_scale)
    watch_grad = spread(groups_a, users, cap_pad, rows, *watch_plan, watch_near, watch_far)
    search_grad = spread(groups_b, users, cap_pad, rows, *search_plan, search_near, search_far)

    cols_one, cols_two, rows_three = weight_one.shape[1], weight_two.shape[1], weight_three.shape[0] // n_tp
    deep = weight_two.shape[0] // 2
    used_rows = weight_one.shape[0] + deep + rows_three + 4
    n_rows = -(-used_rows // (8 * n_dp)) * 8 * n_dp
    small = jnp.sum(g_three, axis=0)

    def weight_block(j):
        t = tp ^ j
        one = lax.dynamic_slice_in_dim(g_one, t * cols_one, cols_one, 1)
        two = lax.dynamic_slice_in_dim(g_two, t * cols_two, cols_two, 1)
        three = lax.dynamic_slice_in_dim(hidden_b, t * rows_three, rows_three, 1)
        grad_two = inner_rows(hidden_a, two)
        return jnp.concatenate(
            [
                inner_rows(feats, one),
                jnp.concatenate([grad_two[:deep], grad_two[deep:]], axis=1),
                inner_rows(three, g_three),
                jnp.sum(one, axis=0)[None, :],
                jnp.pad(jnp.sum(two, axis=0), (0, width - cols_two))[None, :],
                small[None, :],
                jnp.full((1, width), loss_sum, F32),
                jnp.zeros((n_rows - used_rows, width), F32),
            ]
        )

    blocks = [weight_block(j) for j in range(n_tp)]
    for b in range(tp_bits):
        moved = swap(jnp.concatenate(blocks[1::2]), 1 << b, shards)
        blocks = [
            kept + moved[i * n_rows : (i + 1) * n_rows] for i, kept in enumerate(blocks[0::2])
        ]
    total = blocks[0]
    dp_bits = n_dp.bit_length() - 1
    for b in range(dp_bits):
        half = total.shape[0] // 2
        bit = (dp >> b) & 1
        kept = lax.dynamic_slice_in_dim(total, bit * half, half, 0)
        moved = lax.dynamic_slice_in_dim(total, (1 - bit) * half, half, 0)
        total = kept + swap(moved, 1 << (b + tp_bits), shards)
    for b in reversed(range(dp_bits)):
        bit = (dp >> b) & 1
        other = swap(total, 1 << (b + tp_bits), shards)
        total = jnp.concatenate([jnp.where(bit == 0, total, other), jnp.where(bit == 0, other, total)])
    at = weight_one.shape[0]
    w_one_grad = total[:at]
    w_two_grad = jnp.concatenate([total[at : at + deep, :cols_two], total[at : at + deep, cols_two:]])
    at += deep
    w_three_grad = lax.all_gather(total[at : at + rows_three], "tp", axis=0, tiled=True)
    at += rows_three
    b_one_grad = total[at]
    b_two_grad = total[at + 1, :cols_two]
    b_three_grad = total[at + 2]
    mean_loss = total[at + 3, 0] / F32(users * shards)

    pos_from = (jnp.arange(shards, dtype=I32)[:, None] * users + pos_user).reshape(-1)
    g_pos = user_all[pos_from] * coef_all[pos_from][:, None]
    output_grad = jnp.zeros((rows, width), F32).at[pos_row.reshape(-1)].add(g_pos, mode="drop")

    def add_block(i, grad):
        ids = lax.dynamic_slice_in_dim(own_rows_id, i * block, block, 0)
        logq = lax.dynamic_slice_in_dim(own_logq, i * block, block, 0)
        held = out_table[jnp.minimum(ids, rows - 1)]
        scores = matmul_t(held, user_all) - logq[:, None]
        chance = jnp.exp(jnp.where((ids < rows)[:, None], scores - lse_all[None, :], -BIG))
        return grad.at[ids].add(matmul(chance, user_all), mode="drop")

    my_count = jnp.sum(neg_mine.astype(I32))
    output_grad = lax.fori_loop(0, (my_count + block - 1) // block, add_block, output_grad)
    return (
        mean_loss,
        watch_grad,
        search_grad,
        output_grad,
        w_one_grad,
        b_one_grad,
        w_two_grad,
        b_two_grad,
        w_three_grad,
        b_three_grad,
        dense_grad,
    )


def solution(mesh):
    both = P(AXES)
    rows = P(AXES, None)
    in_specs = (
        rows, both, rows, both, both, both, both, P(), P(), rows, rows, rows, rows,
        P(None, "tp"), P("tp"), P(None, "tp"), P("tp"), P(), P(),
    )
    out_specs = (
        P(), rows, rows, rows, P(None, "tp"), P("tp"), P(None, "tp"), P("tp"), P(), P(), rows,
    )
    return jax.shard_map(body, mesh=mesh, in_specs=in_specs, out_specs=out_specs, check_vma=False)
```

time: 2000 us -> 536 us (0.27)
  waiting for transfers between devices: 832 us -> 70.2 us
  local copies, waits for them, and re-layouts: 422 us -> 141 us
  other arithmetic: 342 us -> 73.3 us
  blocking collectives: 252 us -> 75.2 us
  Pallas kernels: 0 us -> 69.2 us
  matrix products: 82.6 us -> 40.2 us
    all_to_all x8 -> x2, waiting for transfers between devices: 522 us -> 0.01 us  [the longest x1 0.01 us: body(): lax.all_to_all(served, AXES, split_axis=0, concat_axis=0, tiled=True)]
    psum x2 -> x0, waiting for transfers between devices: 246 us -> none  [the longest x1 144 us: body(): lax.psum((w_one_grad, b_one_grad, w_two_grad, b_two_grad, w_three_grad, b...]
    psum x1 -> x0, blocking collectives: 228 us -> none  [body(): lax.psum((w_one_grad, b_one_grad, w_two_grad, b_two_grad, w_three_grad, b...]
    scatter-add x4 -> x2, other arithmetic: 160 us -> 11.6 us  [the longest x1 5.86 us: body(): jnp.zeros((rows, width), F32).at[pos_row.reshape(-1)]]
    gather x18 -> x134, local copies, waits for them, and re-layouts: 210 us -> 79.2 us  [the longest x3 67.7 us: buckets(): sorted_owner = owners[order]]
    scatter x3 -> x0, other arithmetic: 106 us -> none  [the longest x1 52.5 us: body(): jnp.zeros((shards * bound_ids, width), jnp.float32).at[watch_slots]]
    scatter x6 -> x0, local copies, waits for them, and re-layouts: 97.7 us -> none  [the longest x3 48.9 us: buckets(): jnp.zeros((count,), jnp.int32).at[order].set(sorted_owner * bound + rank)]
    pallas_call x0 -> x4, Pallas kernels: none -> 69.2 us  [the longest x2 37.9 us: spread(): pl.pallas_call(functools.partial(spread_kernel, groups, users, cap), out_...]
  transfers between devices with their start and end apart: 15 -> 34, of which waited for: 10 -> 13; matrix products, arithmetic and copies ran while one was open for 28% -> 47% of each run, Pallas kernels for 0% -> 13%
where the time goes in v1:
time: 536 us; the launch traced here: 525 us
  local copies, waits for them, and re-layouts  141 us (26%)
  blocking collectives  75.2 us (14%)
  other arithmetic  73.3 us (14%)
  waiting for transfers between devices  70.2 us (13%)
  Pallas kernels  69.2 us (13%)
  matrix products  40.2 us (8%)
  starting transfers between devices  37 us (7%)
  between operations  18.5 us (3%)
    ppermute x28, waiting for transfers between devices, swap(): return lax.ppermute(x, AXES, [(i, i ^ mask) for i in range(shards)])  68.4 us
    gather x128, local copies, waits for them, and re-layouts  66.8 us
    all_gather x1, blocking collectives, body(): stats = lax.all_gather(jnp.stack([lse, coef]), AXES, axis=0, tiled=False)  58.2 us
    pallas_call x2, Pallas kernels, spread(): pl.pallas_call(functools.partial(spread_kernel, groups, users, cap), out_...  37.9 us
    pallas_call x2, Pallas kernels, pool(): pl.pallas_call(functools.partial(pool_kernel, groups, users, cap), out_sh...  31.3 us
    ppermute x28, starting transfers between devices, swap(): return lax.ppermute(x, AXES, [(i, i ^ mask) for i in range(shards)])  22.7 us
    concatenate x1, local copies, waits for them, and re-layouts, body(): moved = swap(jnp.concatenate(blocks[1::2]), 1 << b, shards)  18.1 us
    dot_general x5, matrix products, matmul_t(): lax.dot_general(left, right, (((1,), (1,)), ((), ())), precision=lax.Prec...  16.2 us
  transfers between devices with their start and end apart: 34, of which 13 were waited for; matrix products, arithmetic and copies ran while one was open for 47% of the time, Pallas kernels for 13%

profile of v1, /device:TPU:0, one launch (start us, length us, event | category | flops | bytes accessed | tf_op | source)
XLA Modules:
  0.0 525.3 jit_solution(7687422224717964539)
XLA Ops:
  15.2 11.2 %sort.37 = (s32[19392]{0:T(1024)S(1)}, s32[19392]{0:T(1024)}) sort(s32[19392]{0:T(1024)S(1)} %constant_dynamic-update-slice_fusion.10, s32[19392]{0:T(1024)S(1)} %iota.87), dimensions={0}, to_apply=%region_9.10 | sort | flops 290880 | bytes 310272 | tf_op jit(solution)/shard_map/sort | solution.py:241
  28.2 7.3 %all-to-all-start = ((s32[32,1,1212]{2,1,0:T(1,128)}), s32[32,1,1212]{2,1,0:T(1,128)S(1)}, u32[]{:S(2)}, u32[]{:S(2)}) async-start(s32[32,1,1212]{2,1,0:T(1,128)} %reshape.397), calls=%async_computation | async-start | bytes 327680 | tf_op jit(solution)/shard_map/all_to_all | solution.py:250
  36.3 7.7 %sort.38 = (s32[5000]{0:T(1024)S(1)}, f32[5000]{0:T(1024)S(1)}, s32[5000]{0:T(1024)}) sort(s32[5000]{0:T(1024)S(1)} %fusion.87, f32[5000]{0:T(1024)S(1)} %copy-done.19, s32[5000]{0:T(1024)S(1)} %iota.88), dimensions={0}, to_apply=%region_14.15 | sort | flops 65000 | bytes 120000 | tf_op jit(solution)/shard_map/sort | solution.py:206
  44.6 3.3 gather_fusion.2
  48.8 67.5 %while.24 = (s32[]{:T(128)}, s32[32,1212]{1,0:T(8,128)S(1)}, s32[32,2]{0,1:T(2,128)S(1)}, s32[32,1200]{1,0:T(8,128)S(1)}, s32[]{:T(128)}, /*index=5*/s32[]{:T(128)}) while((s32[]{:T(128)}, s32[32,1212]{1,0:T(8,128)S(1)}, s32[32,2]{0,1:T(2,128)S(1)}, s32[32,1200]{1,0:T(8,128)S(1)}, s32[]{:T(128)}, /*index=5*/s32[]{:T(128)}) %tuple.114), condition=%wide.while_cond, body=%wide.while_body.sunk | while | flops 2 | bytes 19313 | solution.py:255
  118.6 17.0 %shard_map.275 = (f32[2048,2,128]{2,1,0:T(2,128)}, f32[2048,2,128]{2,1,0:T(2,128)}) custom-call(s32[32]{0:T(128)} %get-tuple-element.125.cnt_ref, s32[9600]{0:T(1024)} %reshape.400.idx_ref, f32[4096,256]{1,0:T(8,128)} %tab_ref.2), custom_call_target="tpu_custom_call" | custom-call | bytes 41943040 | tf_op jit(solution)/shard_map/pallas_call | solution.py:86
  137.3 14.3 %shard_map.276 = (f32[2048,2,128]{2,1,0:T(2,128)}, f32[2048,2,128]{2,1,0:T(2,128)}) custom-call(s32[32]{0:T(128)} %get-tuple-element.126.cnt_ref, s32[9600]{0:T(1024)} %reshape.403.idx_ref, f32[4096,256]{1,0:T(8,128)} %tab_ref.3), custom_call_target="tpu_custom_call" | custom-call | bytes 41943040 | tf_op jit(solution)/shard_map/pallas_call | solution.py:86
  152.5 2.5 add.474
  159.6 20.7 %collective-permute-done.1 = f32[1024,2,128]{2,1,0:T(2,128)S(1)} collective-permute-done((f32[1024,2,128]{2,1,0:T(2,128)S(1)}, f32[1024,2,128]{2,1,0:T(2,128)S(1)}, u32[]{:S(2)}, u32[]{:S(2)}) %collective-permute-start.1) | collective-permute-done | bytes 1048608 | tf_op jit(solution)/shard_map/ppermute | solution.py:38
  185.9 3.1 gather_fusion.3
  189.7 6.7 %all-to-all-start.1 = ((f32[32,6,256]{2,1,0:T(8,128)}), f32[32,6,256]{2,1,0:T(8,128)S(1)}, u32[]{:S(2)}, u32[]{:S(2)}) async-start(f32[32,6,256]{2,1,0:T(8,128)} %reshape.458), calls=%async_computation.1 | async-start | bytes 524288 | tf_op jit(solution)/shard_map/all_to_all | solution.py:283
  198.5 1.8 collective-permute-start.3
  203.2 5.0 all-gather.3
  208.3 5.1 all-gather.2
  215.3 4.1 collective-permute-start.4
  219.6 9.2 %collective-permute-done.4 = f32[128,2,128]{2,1,0:T(2,128)S(1)} collective-permute-done((f32[128,2,128]{2,1,0:T(2,128)S(1)}, f32[128,2,128]{2,1,0:T(2,128)S(1)}, u32[]{:S(2)}, u32[]{:S(2)}) %collective-permute-start.4) | collective-permute-done | bytes 131104 | tf_op jit(solution)/shard_map/ppermute | solution.py:38
  229.0 2.6 collective-permute-done.9
  231.8 2.7 convolution_add_fusion
  234.5 2.6 convolution_add_fusion.1
  240.6 7.0 %fusion.137 = (f32[128]{0:T(128)S(1)}, f32[128,6912]{1,0:T(8,128)S(1)}) fusion(f32[6912]{0:T(1024)} %get-tuple-element.107, f32[6912,256]{1,0:T(8,128)} %get-tuple-element.106, f32[128,256]{1,0:T(8,128)S(1)} %get-tuple-element.225), kind=kOutput, calls=%fused_computation.383 | convolution fusion | flops 1360985984 | bytes 10776064 | tf_op jit(solution)/shard_map/dot_general | solution.py:26
  249.5 3.2 fusion.138
  266.4 18.1 %concatenate.93 = f32[2688,256]{1,0:T(8,128)} concatenate(f32[640,256]{1,0:T(8,128)} %fusion.36, f32[512,256]{1,0:T(8,128)} %pad_maximum_fusion.5, f32[128,256]{1,0:T(8,128)} %fusion.45, f32[1,256]{1,0:T(1,128)} %bitcast.110, f32[1,256]{1,0:T(1,128)} %bitcast.112, f32[1,256]{1,0:T(1,128)} %bitcast.98, f32[1,256]{1,0:T(1,128)} %broadcast_in_dim.106, f32[60,256]{1,0:T(8,128)} %broadcast.543, ...), dimensions={0} | concatenate | bytes 5505024 | tf_op jit(solution)/shard_map/concatenate | solution.py:367
  294.2 2.4 fusion.140
  298.8 2.9 collective-permute-start.18
  301.7 1.7 fusion.50
  304.8 1.8 fusion.41
  306.6 3.2 concatenate.95
  309.8 2.6 slice_add_fusion
  319.2 58.2 %all-gather.4 = f32[32,2,128]{2,1,0:T(2,128)S(1)} all-gather(f32[1,2,128]{2,1,0:T(2,128)S(1)} %maximum_bitcast_fusion), channel_id=3, replica_groups=mesh['dp'=8,'tp'=4] {'dp','tp'}, dimensions={0}, use_global_device_ids=true | all-gather | bytes 33792 | tf_op jit(solution)/shard_map/all_gather | solution.py:319
  379.1 2.0 fusion.9
  384.3 5.9 %scatter_custom_fusion.1 = f32[4096,256]{1,0:T(8,128)} fusion(s32[192]{0:T(256)} %bitcast.115, f32[]{:T(128)} %constant.362.clone.1, f32[192]{0:T(256)S(1)} %gather_fusion.5, f32[4096,256]{1,0:T(8,128)} %all-gather.14.cloned.1.call-done, s32[1024]{0:T(1024)S(1)} %pad_clamp_fusion.2), kind=kCustom, calls=%fused_computation.29 | custom fusion | flops 98304 | bytes 8393984 | tf_op jit(solution)/shard_map/scatter-add | solution.py:396
  392.4 2.1 collective-permute-start.19
  397.6 2.8 collective-permute-done.24
  402.0 4.1 collective-permute-done.19
  407.3 2.1 collective-permute-start.20
  410.1 4.4 collective-permute-done.25
  417.5 4.7 collective-permute-done.20
  423.7 2.4 collective-permute-done.14
  427.1 6.0 %collective-permute-done.15 = f32[168,256]{1,0:T(8,128)S(1)} collective-permute-done((f32[168,256]{1,0:T(8,128)S(1)}, f32[168,256]{1,0:T(8,128)S(1)}, u32[]{:S(2)}, u32[]{:S(2)}) %collective-permute-start.15) | collective-permute-done | bytes 172064 | tf_op jit(solution)/shard_map/ppermute | solution.py:38
  433.2 9.3 %collective-permute-done.26 = f32[1024,2,128]{2,1,0:T(2,128)S(1)} collective-permute-done((f32[1024,2,128]{2,1,0:T(2,128)S(1)}, f32[1024,2,128]{2,1,0:T(2,128)S(1)}, u32[]{:S(2)}, u32[]{:S(2)}) %collective-permute-start.26) | collective-permute-done | bytes 1048608 | tf_op jit(solution)/shard_map/ppermute | solution.py:38
  447.0 18.0 %while.23 = (s32[]{:T(128)}, f32[4096,256]{1,0:T(8,128)}, s32[]{:T(128)}, s32[5208]{0:T(1024)}, f32[4096,256]{1,0:T(8,128)}, /*index=5*/f32[4096,256]{1,0:T(8,12...) while((s32[]{:T(128)}, f32[4096,256]{1,0:T(8,128)}, ...), condition=%wide.region_36.37_spmd, body=%wide.region_34.36_spmd.sunk | while | flops 2619857408 | bytes 33501932 | solution.py:407
  447.8 3.1 gather_fusion
  452.4 4.9 fusion.171
  457.4 1.9 fusion.172
  459.2 5.7 %scatter_fusion = f32[4096,256]{1,0:T(8,128)} fusion(f32[4096,256]{1,0:T(8,128)} %get-tuple-element.374, s32[208]{0:T(256)S(1)} %get-tuple-element.314, f32[208,256]{1,0:T(8,128)S(1)} %fusion.172), kind=kCustom, calls=%fused_computation.7.clone.1 | custom fusion | flops 53248 | bytes 639808 | tf_op jit(solution)/shard_map/while/body/scatter-add | solution.py:404
  466.5 16.5 %shard_map.278 = f32[4096,256]{1,0:T(8,128)} custom-call(s32[32]{0:T(128)} %get-tuple-element.126.cnt_ref, s32[9600]{0:T(1024)} %reshape.403.idx_ref, f32[2048,2,128]{2,1,0:T(2,128)} %constant_dynamic-update-slice_fusion.5.near_ref, f32[2048,2,128]{2,1,0:T(2,128)} %collective-permute-done.27.far_ref), custom_call_target="tpu_custom_call" | custom-call | bytes 41943040 | tf_op jit(solution)/shard_map/pallas_call | solution.py:124
  483.0 21.4 %shard_map.277 = f32[4096,256]{1,0:T(8,128)} custom-call(s32[32]{0:T(128)} %get-tuple-element.125.cnt_ref, s32[9600]{0:T(1024)} %reshape.400.idx_ref, f32[2048,2,128]{2,1,0:T(2,128)} %copy-done.6, f32[2048,2,128]{2,1,0:T(2,128)} %collective-permute-done.22.far_ref), custom_call_target="tpu_custom_call" | custom-call | bytes 41943040 | tf_op jit(solution)/shard_map/pallas_call | solution.py:124
  508.9 6.9 %all_gather.39 = f32[512,256]{1,0:T(8,128)S(1)} all-gather(f32[128,256]{1,0:T(8,128)S(1)} %slice.278), channel_id=1, replica_groups=mesh['dp'=8,'tp'=4] {'tp'}, dimensions={0}, use_global_device_ids=true | all-gather | bytes 655360 | tf_op jit(solution)/shard_map/all_gather | solution.py:387
  (452 shorter events, 172.0 us)
Async XLA Ops:
  7.2 229.9 %copy-start = (f32[512,256]{1,0:T(8,128)S(1)}, f32[512,256]{1,0:T(8,128)}, u32[]{:S(2)}) copy-start(f32[512,256]{1,0:T(8,128)} %param.41) | copy-start | bytes 1572868
  7.2 28.4 %copy-start.18 = (s32[5000]{0:T(1024)S(1)}, s32[5000]{0:T(1024)}, u32[]{:S(2)}) copy-start(s32[5000]{0:T(1024)} %param.31) | copy-start | bytes 60004
  7.2 29.1 %copy-start.19 = (f32[5000]{0:T(1024)S(1)}, f32[5000]{0:T(1024)}, u32[]{:S(2)}) copy-start(f32[5000]{0:T(1024)} %param.32) | copy-start | bytes 60004
  7.2 224.6 %all-gather.10.cloned.1.call-start = ((), (), s32[]{:S(2)}) async-start(), calls=%async_computation.3 | async-start | bytes 3276800 | tf_op jit(solution)/shard_map/all_gather | solution.py:225
  7.9 226.6 %all-gather.12.cloned.1.call-start = ((), (), s32[]{:S(2)}) async-start(), calls=%async_computation.4 | async-start | bytes 2621440 | tf_op jit(solution)/shard_map/all_gather | solution.py:226
  10.6 38.1 %copy-start.40 = (s32[32]{0:T(128)S(1)}, s32[32]{0:T(128)}, u32[]{:S(2)}) copy-start(s32[32]{0:T(128)} %constant.378.clone) | copy-start | bytes 388
  28.2 20.5 %all-to-all-start = ((s32[32,1,1212]{2,1,0:T(1,128)}), s32[32,1,1212]{2,1,0:T(1,128)S(1)}, u32[]{:S(2)}, u32[]{:S(2)}) async-start(s32[32,1,1212]{2,1,0:T(1,128)} %reshape.397), calls=%async_computation | async-start | bytes 327680 | tf_op jit(solution)/shard_map/all_to_all | solution.py:250
  35.5 202.6 %all-gather.16.cloned.1.call-start = ((), (), s32[]{:S(2)}) async-start(), calls=%async_computation.6 | async-start | bytes 7299072 | tf_op jit(solution)/shard_map/all_gather | solution.py:218
  135.6 16.8 %collective-permute-start = (f32[2048,2,128]{2,1,0:T(2,128)}, f32[2048,2,128]{2,1,0:T(2,128)}, u32[]{:S(2)}, u32[]{:S(2)}) collective-permute-start(f32[2048,2,128]{2,1,0:T(2,128)} %get-tuple-element.101), channel_id=1, source_target_pairs={{0,1},{1,0},{2,3},{3,2},{4,5},{5,4},{6,7},{7,6},{8,9},{9,8},{10,11... | collective-permute-start | bytes 6291464 | tf_op jit(solution)/shard_map/ppermute | solution.py:38
  137.3 15.2 %copy-start.7 = (f32[2048,2,128]{2,1,0:T(2,128)S(1)}, f32[2048,2,128]{2,1,0:T(2,128)}, u32[]{:S(2)}) copy-start(f32[2048,2,128]{2,1,0:T(2,128)} %get-tuple-element.100) | copy-start | bytes 6291460
  151.6 4.8 collective-permute-start.5
  155.1 25.2 %collective-permute-start.1 = (f32[1024,2,128]{2,1,0:T(2,128)S(1)}, f32[1024,2,128]{2,1,0:T(2,128)S(1)}, u32[]{:S(2)}, u32[]{:S(2)}) collective-permute-start(f32[1024,2,128]{2,1,0:T(2,128)S(1)} %slice.241), channel_id=1, source_target_pairs={{0,2},{1,3},{2,0},{3,1},{4,6},{5,7},{6,4},{7,5},{8,10},{9,11},{10,... | collective-permute-start | bytes 3145736 | tf_op jit(solution)/shard_map/ppermute | solution.py:38
  157.7 25.5 %collective-permute-start.6 = (f32[1024,2,128]{2,1,0:T(2,128)S(1)}, f32[1024,2,128]{2,1,0:T(2,128)S(1)}, u32[]{:S(2)}, u32[]{:S(2)}) collective-permute-start(f32[1024,2,128]{2,1,0:T(2,128)S(1)} %slice.249), channel_id=1, source_target_pairs={{0,4},{1,5},{2,6},{3,7},{4,0},{5,1},{6,2},{7,3},{8,12},{9,13},{10,... | collective-permute-start | bytes 3145736 | tf_op jit(solution)/shard_map/ppermute | solution.py:38
  159.5 69.3 %copy-start.30 = (f32[128]{0:T(128)}, f32[128]{0:T(128)S(1)}, u32[]{:S(2)}) copy-start(f32[128]{0:T(128)S(1)} %get-tuple-element.231) | copy-start | bytes 1540
  159.5 72.1 %copy-start.28 = (f32[128]{0:T(128)}, f32[128]{0:T(128)S(1)}, u32[]{:S(2)}) copy-start(f32[128]{0:T(128)S(1)} %get-tuple-element.230) | copy-start | bytes 1540
  181.6 14.8 %collective-permute-start.2 = (f32[512,2,128]{2,1,0:T(2,128)}, f32[512,2,128]{2,1,0:T(2,128)}, u32[]{:S(2)}, u32[]{:S(2)}) collective-permute-start(f32[512,2,128]{2,1,0:T(2,128)} %slice.243), channel_id=1, source_target_pairs={{0,4},{1,5},{2,6},{3,7},{4,0},{5,1},{6,2},{7,3},{8,12},{9,13},{10,... | collective-permute-start | bytes 1572872 | tf_op jit(solution)/shard_map/ppermute | solution.py:38
  184.6 15.6 %collective-permute-start.7 = (f32[512,2,128]{2,1,0:T(2,128)}, f32[512,2,128]{2,1,0:T(2,128)}, u32[]{:S(2)}, u32[]{:S(2)}) collective-permute-start(f32[512,2,128]{2,1,0:T(2,128)} %slice.251), channel_id=1, source_target_pairs={{0,2},{1,3},{2,0},{3,1},{4,6},{5,7},{6,4},{7,5},{8,10},{9,11},{10,... | collective-permute-start | bytes 1572872 | tf_op jit(solution)/shard_map/ppermute | solution.py:38
  189.0 14.3 %copy-start.38 = (f32[128]{0:T(128)S(1)}, f32[128]{0:T(128)}, u32[]{:S(2)}) copy-start(f32[128]{0:T(128)} %param.40) | copy-start | bytes 1540
  189.0 19.3 %copy-start.36 = (f32[256]{0:T(256)S(1)}, f32[256]{0:T(256)}, u32[]{:S(2)}) copy-start(f32[256]{0:T(256)} %param.38) | copy-start | bytes 3076
  189.7 23.6 %all-to-all-start.1 = ((f32[32,6,256]{2,1,0:T(8,128)}), f32[32,6,256]{2,1,0:T(8,128)S(1)}, u32[]{:S(2)}, u32[]{:S(2)}) async-start(f32[32,6,256]{2,1,0:T(8,128)} %reshape.458), calls=%async_computation.1 | async-start | bytes 524288 | tf_op jit(solution)/shard_map/all_to_all | solution.py:283
  198.5 15.7 %collective-permute-start.3 = (f32[256,2,128]{2,1,0:T(2,128)}, f32[256,2,128]{2,1,0:T(2,128)}, u32[]{:S(2)}, u32[]{:S(2)}) collective-permute-start(f32[256,2,128]{2,1,0:T(2,128)} %slice.245), channel_id=1, source_target_pairs={{0,8},{1,9},{2,10},{3,11},{4,12},{5,13},{6,14},{7,15},{8,0},{9,1},... | collective-permute-start | bytes 786440 | tf_op jit(solution)/shard_map/ppermute | solution.py:38
  201.5 30.2 %copy-start.14 = (f32[128,128]{1,0:T(8,128)S(1)}, f32[128,128]{1,0:T(8,128)}, u32[]{:S(2)}) copy-start(f32[128,128]{1,0:T(8,128)} %param.33) | copy-start | bytes 196612
  201.6 17.7 %collective-permute-start.8 = (f32[256,2,128]{2,1,0:T(2,128)S(1)}, f32[256,2,128]{2,1,0:T(2,128)S(1)}, u32[]{:S(2)}, u32[]{:S(2)}) collective-permute-start(f32[256,2,128]{2,1,0:T(2,128)S(1)} %slice.253), channel_id=1, source_target_pairs={{0,8},{1,9},{2,10},{3,11},{4,12},{5,13},{6,14},{7,15},{8,0},{9,1},... | collective-permute-start | bytes 786440 | tf_op jit(solution)/shard_map/ppermute | solution.py:38
  215.3 13.5 %collective-permute-start.4 = (f32[128,2,128]{2,1,0:T(2,128)S(1)}, f32[128,2,128]{2,1,0:T(2,128)S(1)}, u32[]{:S(2)}, u32[]{:S(2)}) collective-permute-start(f32[128,2,128]{2,1,0:T(2,128)S(1)} %slice.247), channel_id=1, source_target_pairs={{0,16},{1,17},{2,18},{3,19},{4,20},{5,21},{6,22},{7,23},{8,24},{9,... | collective-permute-start | bytes 393224 | tf_op jit(solution)/shard_map/ppermute | solution.py:38
  219.5 12.1 %collective-permute-start.9 = (f32[128,2,128]{2,1,0:T(2,128)S(1)}, f32[128,2,128]{2,1,0:T(2,128)S(1)}, u32[]{:S(2)}, u32[]{:S(2)}) collective-permute-start(f32[128,2,128]{2,1,0:T(2,128)S(1)} %slice.255), channel_id=1, source_target_pairs={{0,16},{1,17},{2,18},{3,19},{4,20},{5,21},{6,22},{7,23},{8,24},{9,... | collective-permute-start | bytes 393224 | tf_op jit(solution)/shard_map/ppermute | solution.py:38
  234.5 24.1 %copy-start.10 = (f32[128,1024]{1,0:T(8,128)}, f32[128,1024]{1,0:T(8,128)S(1)}, u32[]{:S(2)}) copy-start(f32[128,1024]{1,0:T(8,128)S(1)} %convolution_add_fusion) | copy-start | bytes 1572868
  240.0 144.3 %all-gather.14.cloned.1.call-start = ((), (), s32[]{:S(2)}) async-start(), calls=%async_computation.5 | async-start | bytes 4325376 | tf_op jit(solution)/shard_map/all_gather | solution.py:308
  253.2 10.4 %copy-start.20 = (f32[128,512]{1,0:T(8,128)}, f32[128,512]{1,0:T(8,128)S(1)}, u32[]{:S(2)}) copy-start(f32[128,512]{1,0:T(8,128)S(1)} %get-tuple-element.194) | copy-start | bytes 786436
  266.4 27.7 %copy-start.2 = (f32[640,1024]{1,0:T(8,128)S(1)}, f32[640,1024]{1,0:T(8,128)}, u32[]{:S(2)}) copy-start(f32[640,1024]{1,0:T(8,128)} %all-gather.10.cloned.1.call-done) | copy-start | bytes 7864324
  284.5 25.3 %collective-permute-start.10 = (f32[2688,256]{1,0:T(8,128)}, f32[2688,256]{1,0:T(8,128)}, u32[]{:S(2)}, u32[]{:S(2)}) collective-permute-start(f32[2688,256]{1,0:T(8,128)} %concatenate.93), channel_id=1, source_target_pairs={{0,1},{1,0},{2,3},{3,2},{4,5},{5,4},{6,7},{7,6},{8,9},{9,8},{10,11... | collective-permute-start | bytes 8257544 | tf_op jit(solution)/shard_map/ppermute | solution.py:38
  298.1 92.1 %collective-permute-start.23 = (f32[128,2,128]{2,1,0:T(2,128)}, f32[128,2,128]{2,1,0:T(2,128)}, u32[]{:S(2)}, u32[]{:S(2)}) collective-permute-start(f32[128,2,128]{2,1,0:T(2,128)} %reshape.411), channel_id=1, source_target_pairs={{0,16},{1,17},{2,18},{3,19},{4,20},{5,21},{6,22},{7,23},{8,24},{9,... | collective-permute-start | bytes 393224 | tf_op jit(solution)/shard_map/ppermute | solution.py:38
  298.8 92.5 %collective-permute-start.18 = (f32[128,2,128]{2,1,0:T(2,128)}, f32[128,2,128]{2,1,0:T(2,128)}, u32[]{:S(2)}, u32[]{:S(2)}) collective-permute-start(f32[128,2,128]{2,1,0:T(2,128)} %reshape.410), channel_id=1, source_target_pairs={{0,16},{1,17},{2,18},{3,19},{4,20},{5,21},{6,22},{7,23},{8,24},{9,... | collective-permute-start | bytes 393224 | tf_op jit(solution)/shard_map/ppermute | solution.py:38
  312.5 66.6 %collective-permute-start.11 = (f32[1344,256]{1,0:T(8,128)}, f32[1344,256]{1,0:T(8,128)}, u32[]{:S(2)}, u32[]{:S(2)}) collective-permute-start(f32[1344,256]{1,0:T(8,128)} %slice_add_fusion), channel_id=1, source_target_pairs={{0,2},{1,3},{2,0},{3,1},{4,6},{5,7},{6,4},{7,5},{8,10},{9,11},{10,... | collective-permute-start | bytes 4128776 | tf_op jit(solution)/shard_map/ppermute | solution.py:38
  381.2 20.6 %collective-permute-start.12 = (f32[672,256]{1,0:T(8,128)S(1)}, f32[672,256]{1,0:T(8,128)S(1)}, u32[]{:S(2)}, u32[]{:S(2)}) collective-permute-start(f32[672,256]{1,0:T(8,128)S(1)} %constant_dynamic-slice_fusion.3), channel_id=1, source_target_pairs={{0,4},{1,5},{2,6},{3,7},{4,0},{5,1},{6,2},{7,3},{8,12},{9,13},{10,... | collective-permute-start | bytes 2064392 | tf_op jit(solution)/shard_map/ppermute | solution.py:38
  391.3 9.2 %collective-permute-start.24 = (f32[256,2,128]{2,1,0:T(2,128)S(1)}, f32[256,2,128]{2,1,0:T(2,128)S(1)}, u32[]{:S(2)}, u32[]{:S(2)}) collective-permute-start(f32[256,2,128]{2,1,0:T(2,128)S(1)} %pad_maximum_fusion.13), channel_id=1, source_target_pairs={{0,8},{1,9},{2,10},{3,11},{4,12},{5,13},{6,14},{7,15},{8,0},{9,1},... | collective-permute-start | bytes 786440 | tf_op jit(solution)/shard_map/ppermute | solution.py:38
  392.4 13.6 %collective-permute-start.19 = (f32[256,2,128]{2,1,0:T(2,128)S(1)}, f32[256,2,128]{2,1,0:T(2,128)S(1)}, u32[]{:S(2)}, u32[]{:S(2)}) collective-permute-start(f32[256,2,128]{2,1,0:T(2,128)S(1)} %pad_maximum_fusion.12), channel_id=1, source_target_pairs={{0,8},{1,9},{2,10},{3,11},{4,12},{5,13},{6,14},{7,15},{8,0},{9,1},... | collective-permute-start | bytes 786440 | tf_op jit(solution)/shard_map/ppermute | solution.py:38
  401.6 12.8 %collective-permute-start.25 = (f32[512,2,128]{2,1,0:T(2,128)S(1)}, f32[512,2,128]{2,1,0:T(2,128)S(1)}, u32[]{:S(2)}, u32[]{:S(2)}) collective-permute-start(f32[512,2,128]{2,1,0:T(2,128)S(1)} %pad_maximum_fusion.9), channel_id=1, source_target_pairs={{0,2},{1,3},{2,0},{3,1},{4,6},{5,7},{6,4},{7,5},{8,10},{9,11},{10,... | collective-permute-start | bytes 1572872 | tf_op jit(solution)/shard_map/ppermute | solution.py:38
  401.9 15.5 %collective-permute-start.13 = (f32[336,256]{1,0:T(8,128)S(1)}, f32[336,256]{1,0:T(8,128)S(1)}, u32[]{:S(2)}, u32[]{:S(2)}) collective-permute-start(f32[336,256]{1,0:T(8,128)S(1)} %constant_dynamic-slice_fusion.2), channel_id=1, source_target_pairs={{0,8},{1,9},{2,10},{3,11},{4,12},{5,13},{6,14},{7,15},{8,0},{9,1},... | collective-permute-start | bytes 1032200 | tf_op jit(solution)/shard_map/ppermute | solution.py:38
  407.3 15.0 %collective-permute-start.20 = (f32[512,2,128]{2,1,0:T(2,128)S(1)}, f32[512,2,128]{2,1,0:T(2,128)S(1)}, u32[]{:S(2)}, u32[]{:S(2)}) collective-permute-start(f32[512,2,128]{2,1,0:T(2,128)S(1)} %pad_maximum_fusion.8), channel_id=1, source_target_pairs={{0,4},{1,5},{2,6},{3,7},{4,0},{5,1},{6,2},{7,3},{8,12},{9,13},{10,... | collective-permute-start | bytes 1572872 | tf_op jit(solution)/shard_map/ppermute | solution.py:38
  410.1 16.1 %copy-start.5 = (f32[2048,2,128]{2,1,0:T(2,128)S(1)}, f32[2048,2,128]{2,1,0:T(2,128)}, u32[]{:S(2)}) copy-start(f32[2048,2,128]{2,1,0:T(2,128)} %constant_dynamic-update-slice_fusion.3) | copy-start | bytes 6291460
  415.9 26.7 %collective-permute-start.26 = (f32[1024,2,128]{2,1,0:T(2,128)S(1)}, f32[1024,2,128]{2,1,0:T(2,128)S(1)}, u32[]{:S(2)}, u32[]{:S(2)}) collective-permute-start(f32[1024,2,128]{2,1,0:T(2,128)S(1)} %pad_maximum_fusion.1), channel_id=1, source_target_pairs={{0,4},{1,5},{2,6},{3,7},{4,0},{5,1},{6,2},{7,3},{8,12},{9,13},{10,... | collective-permute-start | bytes 3145736 | tf_op jit(solution)/shard_map/ppermute | solution.py:38
  417.4 8.6 %collective-permute-start.14 = (f32[168,256]{1,0:T(8,128)S(1)}, f32[168,256]{1,0:T(8,128)S(1)}, u32[]{:S(2)}, u32[]{:S(2)}) collective-permute-start(f32[168,256]{1,0:T(8,128)S(1)} %constant_dynamic-slice_fusion.1), channel_id=1, source_target_pairs={{0,16},{1,17},{2,18},{3,19},{4,20},{5,21},{6,22},{7,23},{8,24},{9,... | collective-permute-start | bytes 516104 | tf_op jit(solution)/shard_map/ppermute | solution.py:38
  423.6 20.9 %collective-permute-start.21 = (f32[1024,2,128]{2,1,0:T(2,128)S(1)}, f32[1024,2,128]{2,1,0:T(2,128)S(1)}, u32[]{:S(2)}, u32[]{:S(2)}) collective-permute-start(f32[1024,2,128]{2,1,0:T(2,128)S(1)} %pad_maximum_fusion), channel_id=1, source_target_pairs={{0,2},{1,3},{2,0},{3,1},{4,6},{5,7},{6,4},{7,5},{8,10},{9,11},{10,... | collective-permute-start | bytes 3145736 | tf_op jit(solution)/shard_map/ppermute | solution.py:38
  426.1 6.9 %collective-permute-start.15 = (f32[168,256]{1,0:T(8,128)S(1)}, f32[168,256]{1,0:T(8,128)S(1)}, u32[]{:S(2)}, u32[]{:S(2)}) collective-permute-start(f32[168,256]{1,0:T(8,128)S(1)} %dynamic-slice_add_fusion.2), channel_id=1, source_target_pairs={{0,16},{1,17},{2,18},{3,19},{4,20},{5,21},{6,22},{7,23},{8,24},{9,... | collective-permute-start | bytes 516104 | tf_op jit(solution)/shard_map/ppermute | solution.py:38
  433.1 11.7 %collective-permute-start.16 = (f32[336,256]{1,0:T(8,128)S(1)}, f32[336,256]{1,0:T(8,128)S(1)}, u32[]{:S(2)}, u32[]{:S(2)}) collective-permute-start(f32[336,256]{1,0:T(8,128)S(1)} %pad_maximum_fusion.10), channel_id=1, source_target_pairs={{0,8},{1,9},{2,10},{3,11},{4,12},{5,13},{6,14},{7,15},{8,0},{9,1},... | collective-permute-start | bytes 1032200 | tf_op jit(solution)/shard_map/ppermute | solution.py:38
  443.6 22.9 %collective-permute-start.27 = (f32[2048,2,128]{2,1,0:T(2,128)}, f32[2048,2,128]{2,1,0:T(2,128)}, u32[]{:S(2)}, u32[]{:S(2)}) collective-permute-start(f32[2048,2,128]{2,1,0:T(2,128)} %constant_dynamic-update-slice_fusion.5.near_ref), channel_id=1, source_target_pairs={{0,1},{1,0},{2,3},{3,2},{4,5},{5,4},{6,7},{7,6},{8,9},{9,8},{10,11... | collective-permute-start | bytes 6291464 | tf_op jit(solution)/shard_map/ppermute | solution.py:38
  444.7 38.2 %collective-permute-start.22 = (f32[2048,2,128]{2,1,0:T(2,128)S(1)}, f32[2048,2,128]{2,1,0:T(2,128)}, u32[]{:S(2)}, u32[]{:S(2)}) collective-permute-start(f32[2048,2,128]{2,1,0:T(2,128)S(1)} %constant_dynamic-update-slice_fusion.near_ref), channel_id=1, source_target_pairs={{0,1},{1,0},{2,3},{3,2},{4,5},{5,4},{6,7},{7,6},{8,9},{9,8},{10,11... | collective-permute-start | bytes 6291464 | tf_op jit(solution)/shard_map/ppermute | solution.py:38
  446.0 58.3 %collective-permute-start.17 = (f32[672,256]{1,0:T(8,128)}, f32[672,256]{1,0:T(8,128)}, u32[]{:S(2)}, u32[]{:S(2)}) collective-permute-start(f32[672,256]{1,0:T(8,128)} %pad_maximum_fusion.2), channel_id=1, source_target_pairs={{0,4},{1,5},{2,6},{3,7},{4,0},{5,1},{6,2},{7,3},{8,12},{9,13},{10,... | collective-permute-start | bytes 2064392 | tf_op jit(solution)/shard_map/ppermute | solution.py:38
  (29 other events, 152.0 us)
Sparse Core Ops, SparseCore 0:
  9.6 28.3 all-gather.9
  39.5 22.8 all-gather.11
  65.4 74.9 all-gather.15
  243.4 69.2 all-gather.13

commit v2 on v1

v2 whole, which is shorter than its diff:
```python
import functools

import jax
import jax.numpy as jnp
from jax import lax
from jax.experimental import pallas as pl
from jax.experimental.pallas import tpu as pltpu
from jax.sharding import PartitionSpec as P

AXES = ("dp", "tp")
F32 = jnp.float32
I32 = jnp.int32
BIG = 1e30
LANES = 128
GROUP = 4
UNROLL = 8
SHIFT = 9
PAD_ROWS = 8
PARTS = 4
PIECES = 4


def matmul(left, right):
    return jnp.dot(left, right, precision=lax.Precision.HIGH, preferred_element_type=F32)


def matmul_t(left, right):
    return lax.dot_general(
        left, right, (((1,), (1,)), ((), ())), precision=lax.Precision.HIGH, preferred_element_type=F32
    )


def inner_rows(left, right):
    return lax.dot_general(
        left, right, (((0,), (0,)), ((), ())), precision=lax.Precision.HIGH, preferred_element_type=F32
    )


def swap(x, mask, shards):
    return lax.ppermute(x, AXES, [(i, i ^ mask) for i in range(shards)])


def after(x, *earlier):
    return lax.optimization_barrier((x, *earlier))[0]


def exchange(moves, shards, beside=()):
    held = lax.optimization_barrier(tuple(x for x, *_ in moves))
    got = tuple(swap(x, sum(1 << b for b in move[1:]), shards) for x, move in zip(held, moves, strict=True))
    return lax.optimization_barrier(got + tuple(beside))


def places(order):
    n = len(order)
    return [sum(((p >> (n - 1 - j)) & 1) << order[j] for j in range(n)) for p in range(1 << n)]


def group_bounds(me_ref, cnt_ref, members, cap):
    owners = [me_ref[0] ^ q for q in members]
    most = cnt_ref[owners[0]]
    for owner in owners[1:]:
        most = jnp.maximum(most, cnt_ref[owner])
    return [owner * cap for owner in owners], (most + UNROLL - 1) // UNROLL


def pool_kernel(places, users, cap, me_ref, cnt_ref, idx_ref, tab_ref, send_ref, keep_ref, tab, raw, sems):
    rows = tab_ref.shape[0]
    part = rows // PARTS
    copies = [
        pltpu.make_async_copy(tab_ref.at[pl.ds(n * part, part)], raw.at[pl.ds(n * part, part)], sems.at[n])
        for n in range(PARTS)
    ]
    for copy in copies:
        copy.start()
    tab[pl.ds(2 * rows, 2 * PAD_ROWS), :] = jnp.zeros((2 * PAD_ROWS, LANES), F32)
    send_ref[...] = jnp.zeros_like(send_ref)
    keep_ref[...] = jnp.zeros_like(keep_ref)
    for n, copy in enumerate(copies):
        copy.wait()
        for h in range(2):
            tab[pl.ds(2 * n * part + h, part, 2), :] = raw[pl.ds(n * part, part), h * LANES : (h + 1) * LANES]
    half = len(places) // 2
    for start in range(0, len(places), GROUP):
        out = keep_ref if start < half else send_ref
        first = (start % half) * 2 * users
        bases, steps = group_bounds(me_ref, cnt_ref, places[start : start + GROUP], cap)

        def step(i, carry, out=out, first=first, bases=bases):
            picks = [[idx_ref[base + (i * UNROLL + u)] for base in bases] for u in range(UNROLL)]
            source = [[tab[pl.ds(pl.multiple_of(v >> SHIFT, 2), 2), :] for v in row] for row in picks]
            for u in range(UNROLL):
                where = [
                    pl.ds(pl.multiple_of(first + k * 2 * users + (v & ((1 << SHIFT) - 1)), 2), 2)
                    for k, v in enumerate(picks[u])
                ]
                held = [out[w, :] for w in where]
                for k in range(GROUP):
                    out[where[k], :] = held[k] + source[u][k]
            return carry

        lax.fori_loop(0, steps, step, 0)


def pool(places, users, cap, me, counts, index, table):
    rows, width = table.shape
    shards = len(places)
    size = 4 * width * (2 * rows + shards * users)
    return pl.pallas_call(
        functools.partial(pool_kernel, places, users, cap),
        out_shape=[jax.ShapeDtypeStruct((shards * users, LANES), F32)] * 2,
        in_specs=[pl.BlockSpec(memory_space=pltpu.SMEM)] * 3 + [pl.BlockSpec(memory_space=pltpu.HBM)],
        out_specs=[pl.BlockSpec(memory_space=pltpu.VMEM)] * 2,
        scratch_shapes=[
            pltpu.VMEM((2 * (rows + PAD_ROWS), LANES), F32),
            pltpu.VMEM((rows, width), F32),
            pltpu.SemaphoreType.DMA((PARTS,)),
        ],
        compiler_params=pltpu.CompilerParams(vmem_limit_bytes=size + (4 << 20)),
        cost_estimate=pl.CostEstimate(flops=0, bytes_accessed=40 << 20, transcendentals=0),
    )(me, counts, index, table)


def spread_kernel(places, users, cap, me_ref, cnt_ref, idx_ref, *refs):
    sources, out_ref, accs = refs[:PIECES], refs[PIECES], refs[PIECES + 1 :]
    rows = out_ref.shape[0]
    for acc in accs:
        acc[...] = jnp.zeros_like(acc)
    piece = len(places) // PIECES
    for start in range(0, len(places), GROUP):
        source_ref = sources[start // piece]
        first = (start % piece) * 2 * users
        bases, steps = group_bounds(me_ref, cnt_ref, places[start : start + GROUP], cap)

        def step(i, carry, source_ref=source_ref, first=first, bases=bases):
            picks = [[idx_ref[base + (i * UNROLL + u)] for base in bases] for u in range(UNROLL)]
            source = [
                [
                    source_ref[pl.ds(pl.multiple_of(first + k * 2 * users + (v & ((1 << SHIFT) - 1)), 2), 2), :]
                    for k, v in enumerate(row)
                ]
                for row in picks
            ]
            for u in range(UNROLL):
                for k in range(0, GROUP, len(accs)):
                    where = [pl.ds(pl.multiple_of(v >> SHIFT, 2), 2) for v in picks[u][k : k + len(accs)]]
                    held = [acc[w, :] for acc, w in zip(accs, where, strict=True)]
                    for n, acc in enumerate(accs):
                        acc[where[n], :] = held[n] + source[u][k + n]
            return carry

        lax.fori_loop(0, steps, step, 0)
    for h in range(2):
        out_ref[:, h * LANES : (h + 1) * LANES] = sum(acc[pl.ds(h, rows, 2), :] for acc in accs)


def spread(places, users, cap, rows, me, counts, index, *sources):
    width = 2 * LANES
    size = 4 * width * (3 * rows + 2 * sources[0].shape[0])
    return pl.pallas_call(
        functools.partial(spread_kernel, places, users, cap),
        out_shape=jax.ShapeDtypeStruct((rows, width), F32),
        in_specs=[pl.BlockSpec(memory_space=pltpu.SMEM)] * 3 + [pl.BlockSpec(memory_space=pltpu.VMEM)] * PIECES,
        out_specs=pl.BlockSpec(memory_space=pltpu.VMEM),
        scratch_shapes=[pltpu.VMEM((2 * (rows + PAD_ROWS), LANES), F32)] * 2,
        compiler_params=pltpu.CompilerParams(vmem_limit_bytes=size + (4 << 20)),
        cost_estimate=pl.CostEstimate(flops=0, bytes_accessed=40 << 20, transcendentals=0),
    )(me, counts, index, *sources)


def split(x):
    high = x.astype(jnp.bfloat16)
    return high, (x - high.astype(F32)).astype(jnp.bfloat16)


def weight_kernel(order, tp_ref, loss_ref, *refs):
    count = (len(refs) - 2) // 2
    out_ref, held, sems = refs[count], refs[count + 1 : -1], refs[-1]
    copies = [pltpu.make_async_copy(refs[n], held[n], sems.at[n]) for n in range(count)]
    for copy in copies:
        copy.start()
    for copy in copies:
        copy.wait()
    f_own, f_rest, a_own, a_rest, b_own, b_rest, grad_ref = held
    n_tp = len(order)
    width = out_ref.shape[1]
    cols_two = grad_ref.shape[2] - 2 * width
    n_feats, n_deep, rows_three = f_own.shape[1], a_own.shape[1] // 2, b_own.shape[1] // n_tp

    def turned(own, rest, lo, size):
        return split(jnp.concatenate([own[:, pl.ds(lo, size)].T, rest[:, pl.ds(lo, size)].T], axis=1))

    def picked(lo, size):
        return split(jnp.concatenate([grad_ref[tp_ref[0] ^ r, :, lo : lo + size] for r in order]))

    def product(left, right):
        (l_high, l_low), (r_high, r_low) = left, right
        return (
            jnp.dot(l_high, r_high, preferred_element_type=F32)
            + jnp.dot(l_low, r_high, preferred_element_type=F32)
            + jnp.dot(l_high, r_low, preferred_element_type=F32)
        )

    one, two, three = picked(0, width), picked(width, cols_two), picked(width + cols_two, width)
    out_ref[:n_feats, :] = product(turned(f_own, f_rest, 0, n_feats), one)
    for h in range(2):
        out_ref[n_feats : n_feats + n_deep, h * cols_two : (h + 1) * cols_two] = product(
            turned(a_own, a_rest, h * n_deep, n_deep), two
        )
    at = n_feats + n_deep
    mine = pl.multiple_of(tp_ref[0] * rows_three, LANES)
    out_ref[at : at + rows_three, :] = product(turned(b_own, b_rest, mine, rows_three), three)
    at += rows_three
    sums = sum(jnp.sum(grad_ref[k], axis=0, keepdims=True) for k in range(n_tp))
    rest = out_ref.shape[0] - at
    out_ref[at:, :] = jnp.concatenate(
        [
            sums[:, :width],
            jnp.concatenate([sums[:, width : width + cols_two], jnp.zeros((1, width - cols_two), F32)], axis=1),
            sums[:, width + cols_two :],
            jnp.full((1, width), loss_ref[0], F32),
            jnp.zeros((rest - 4, width), F32),
        ]
    )


def weight_block(order, n_rows, width, tp, loss, *arrays):
    return pl.pallas_call(
        functools.partial(weight_kernel, order),
        out_shape=jax.ShapeDtypeStruct((n_rows, width), F32),
        in_specs=[pl.BlockSpec(memory_space=pltpu.SMEM)] * 2 + [pl.BlockSpec(memory_space=pltpu.HBM)] * len(arrays),
        out_specs=pl.BlockSpec(memory_space=pltpu.VMEM),
        scratch_shapes=[pltpu.VMEM(x.shape, F32) for x in arrays] + [pltpu.SemaphoreType.DMA((len(arrays),))],
        compiler_params=pltpu.CompilerParams(vmem_limit_bytes=32 << 20),
        cost_estimate=pl.CostEstimate(flops=0, bytes_accessed=16 << 20, transcendentals=0),
    )(tp, loss, *arrays)


def output_kernel(
    users, block, cap_pos, cnt_ref, id_ref, place_ref, logq_ref, pos_ref, pos_user_ref, user_hbm, tab_hbm,
    out_ref, held, logq, acc, user_ref, tab_ref, scaled, sems,
):
    rows = out_ref.shape[0]
    shards = user_ref.shape[0]
    chunk = 4
    tab_copy = pltpu.make_async_copy(tab_hbm, tab_ref, sems.at[0])
    user_copy = pltpu.make_async_copy(user_hbm, user_ref, sems.at[1])
    user_copy.start()
    tab_copy.start()
    out_ref[...] = jnp.zeros_like(out_ref)
    scaled[pl.ds(users, 8), :] = jnp.zeros((8, scaled.shape[1]), F32)
    user_copy.wait()

    def add_pos(s, carry):
        coef = jnp.broadcast_to(user_ref[s, pl.ds(users, 1), users : 2 * users], (LANES, users)).T
        for h in range(scaled.shape[1] // LANES):
            scaled[:users, h * LANES : (h + 1) * LANES] = user_ref[s, :users, h * LANES : (h + 1) * LANES] * coef
        for k in range(cap_pos):
            row = pos_ref[s * cap_pos + k]
            source = jnp.where(row < rows, pos_user_ref[s * cap_pos + k], users)
            at = pl.ds(jnp.minimum(row, rows - 1), 1)
            out_ref[at, :] = out_ref[at, :] + scaled[pl.ds(source, 1), :]
        return carry

    lax.fori_loop(0, shards, add_pos, 0)
    tab_copy.wait()
    count = cnt_ref[0]

    def add_block(r, carry):
        base = r * block

        def fetch(k, carry):
            row = id_ref[base + k]
            held[pl.ds(k, 1), :] = tab_ref[pl.ds(jnp.minimum(row, rows - 1), 1), :]
            q = jnp.where(row < rows, logq_ref[place_ref[base + k]], F32(BIG))
            logq[pl.ds(k, 1), :] = jnp.full((1, LANES), q, F32)
            return carry

        lax.fori_loop(0, block, fetch, 0, unroll=8)
        acc[...] = jnp.zeros_like(acc)
        held_high, held_low = split(held[...])

        def over_users(c, carry):
            parts = [user_ref[c * chunk + j, :users, :] for j in range(chunk)]
            lse = jnp.concatenate(
                [user_ref[c * chunk + j, pl.ds(users, 1), :users] for j in range(chunk)], axis=1
            )
            high, low = split(jnp.concatenate(parts))
            nt = (((1,), (1,)), ((), ()))
            score = (
                lax.dot_general(held_high, high, nt, preferred_element_type=F32)
                + lax.dot_general(held_low, high, nt, preferred_element_type=F32)
                + lax.dot_general(held_high, low, nt, preferred_element_type=F32)
            )
            q = jnp.concatenate([logq[...]] * (chunk * users // LANES), axis=1)
            p_high, p_low = split(jnp.exp(score - q - lse))
            acc[...] += (
                jnp.dot(p_high, high, preferred_element_type=F32)
                + jnp.dot(p_low, high, preferred_element_type=F32)
                + jnp.dot(p_high, low, preferred_element_type=F32)
            )
            return carry

        lax.fori_loop(0, shards // chunk, over_users, 0)

        def put(k, carry):
            at = pl.ds(id_ref[base + k], 1)
            out_ref[at, :] = out_ref[at, :] + acc[pl.ds(k, 1), :]
            return carry

        lax.fori_loop(0, jnp.minimum(block, count - base), put, 0)
        return carry

    lax.fori_loop(0, (count + block - 1) // block, add_block, 0)


def output_rows(users, block, cap_pos, count, ids, places, logq_neg, pos_row, pos_user, user_rows, table):
    rows, width = table.shape
    size = 4 * (2 * rows * width + user_rows.size + 4 * block * width)
    return pl.pallas_call(
        functools.partial(output_kernel, users, block, cap_pos),
        out_shape=jax.ShapeDtypeStruct((rows, width), F32),
        in_specs=[pl.BlockSpec(memory_space=pltpu.SMEM)] * 6 + [pl.BlockSpec(memory_space=pltpu.HBM)] * 2,
        out_specs=pl.BlockSpec(memory_space=pltpu.VMEM),
        scratch_shapes=[
            pltpu.VMEM((block, width), F32),
            pltpu.VMEM((block, LANES), F32),
            pltpu.VMEM((block, width), F32),
            pltpu.VMEM(user_rows.shape, F32),
            pltpu.VMEM(table.shape, F32),
            pltpu.VMEM((users + 8, width), F32),
            pltpu.SemaphoreType.DMA((2,)),
        ],
        compiler_params=pltpu.CompilerParams(vmem_limit_bytes=size + (8 << 20)),
        cost_estimate=pl.CostEstimate(flops=0, bytes_accessed=40 << 20, transcendentals=0),
    )(count, ids, places, logq_neg, pos_row, pos_user, user_rows, table)


def shard_counts(owners, shards):
    return jnp.sum((owners[:, None] == jnp.arange(shards, dtype=I32)[None, :]).astype(I32), axis=0)


def fill_owners(owners, shards, cap):
    lack = cap - shard_counts(owners, shards)
    ends = jnp.sum(jnp.where(jnp.tri(shards, dtype=jnp.bool_), lack[None, :], 0), axis=1)
    extra = jnp.arange(shards * cap - owners.shape[0], dtype=I32)
    return jnp.sum((extra[:, None] >= ends[None, :]).astype(I32), axis=1)


def request_keys(table, ids, used, user, users, rows, shards, cap):
    owner = lax.div(ids, I32(rows))
    unit = rows * users
    real = ((table * shards + owner) * 2 + (1 - used)) * unit + lax.rem(ids, I32(rows)) * users + user
    extra = ((table * shards + fill_owners(owner, shards, cap)) * 2 + 1) * unit
    return [real, extra]


def decode_keys(keys, users, rows):
    used = lax.rem(lax.div(keys, I32(rows * users)), I32(2)) == 0
    row = lax.rem(lax.div(keys, I32(users)), I32(rows))
    return jnp.where(used, row, rows), jnp.where(used, lax.rem(keys, I32(users)), 0)


def body(
    watch_ids,
    watch_len,
    search_ids,
    search_len,
    search_mask,
    positive_ids,
    logq_pos,
    negative_ids,
    logq_neg,
    dense_feats,
    watch_table,
    search_table,
    out_table,
    weight_one,
    bias_one,
    weight_two,
    bias_two,
    weight_three,
    bias_three,
):
    shards = lax.axis_size(AXES)
    n_tp = lax.axis_size("tp")
    n_dp = shards // n_tp
    mine = lax.axis_index(AXES)
    tp = lax.axis_index("tp")
    dp = lax.axis_index("dp")
    bits = shards.bit_length() - 1
    tp_bits = n_tp.bit_length() - 1
    rows, width = watch_table.shape
    users, bag = watch_ids.shape
    negs = negative_ids.shape[0]
    cap = max(2, 3 * users * bag // (2 * shards))
    cap_pos = max(2, 3 * users // (2 * shards))
    cap_pad = -(-cap // UNROLL) * UNROLL
    order_a = list(range(bits))
    order_b = [0, 2, 1] + list(range(3, bits))
    place_a, place_b = places(order_a), places(order_b)
    me = mine.astype(I32).reshape(1)

    neg_owner = lax.div(negative_ids, I32(rows))
    neg_mine = neg_owner == mine
    neg_local = lax.rem(negative_ids, I32(rows))
    neg_span = 1 << (negs - 1).bit_length()
    mean = negs / shards
    block = min(-(-negs // 8) * 8, max(8, int(mean + 4.2 * mean**0.5) // 8 * 8))
    neg_keys = lax.sort(jnp.where(neg_mine, neg_local, rows) * neg_span + jnp.arange(negs, dtype=I32))
    own_rows_id = jnp.pad(lax.div(neg_keys, I32(neg_span)), (0, block), constant_values=rows)
    own_place = jnp.pad(lax.rem(neg_keys, I32(neg_span)), (0, block))
    first_id = own_rows_id[:block]
    first_logq = logq_neg[own_place[:block]]
    logq_rows = -(-block // (8 * width)) * 8
    payload = jnp.concatenate(
        [
            out_table[jnp.minimum(first_id, rows - 1)],
            jnp.pad(first_logq, (0, logq_rows * width - block)).reshape(logq_rows, width),
        ]
    )
    side_bit = tp_bits - 1
    side = (mine >> side_bit) & 1
    side_order = [b for b in reversed(range(bits)) if b != side_bit]
    side_places = jnp.array(
        [sum(((p >> k) & 1) << b for k, b in enumerate(side_order)) for p in range(1 << len(side_order))], I32
    )

    n_feats, cols_two = weight_one.shape[0], weight_two.shape[1]
    bias_pad = 8
    bias_rows = jnp.stack([bias_one, jnp.pad(bias_two, (0, width - cols_two))])
    w_one = jnp.concatenate([weight_one, jnp.pad(bias_rows, ((0, bias_pad - 2), (0, 0)))])
    w_one = lax.all_gather(w_one, "tp", axis=1, tiled=True)
    w_two = lax.all_gather(weight_two, "tp", axis=1, tiled=True)
    deep = weight_two.shape[0] // 2

    slot = jnp.arange(users * bag, dtype=I32)
    slot_user = lax.div(slot, I32(bag))
    spot = jnp.arange(bag, dtype=I32)[None, :]
    watch_used = (spot < watch_len[:, None]).astype(I32).reshape(-1)
    search_used = ((spot < search_len[:, None]) & (search_mask[:, None] > 0)).astype(I32).reshape(-1)
    user_index = jnp.arange(users, dtype=I32)
    keys = jnp.concatenate(
        request_keys(0, watch_ids.reshape(-1), watch_used, slot_user, users, rows, shards, cap)
        + request_keys(1, search_ids.reshape(-1), search_used, slot_user, users, rows, shards, cap)
        + request_keys(2, positive_ids, 1, user_index, users, rows, shards, cap_pos)
    )
    keys, payload = lax.optimization_barrier((keys, payload))
    moved, keys, w_one = exchange([(payload, side_order[0])], shards, [lax.sort(keys), w_one])
    b_one = w_one[n_feats]
    b_two = w_one[n_feats + 1].reshape(n_tp, width)[:, :cols_two].reshape(-1)
    side_rows = jnp.concatenate([payload, moved])
    ends = [shards * cap, 2 * shards * cap, shards * (2 * cap + cap_pos)]
    parts = [
        keys[: ends[0]].reshape(shards, cap),
        keys[ends[0] : ends[1]].reshape(shards, cap),
        keys[ends[1] : ends[2]].reshape(shards, cap_pos),
    ]
    decoded = [piece for part in parts for piece in decode_keys(part, users, rows)]
    request = jnp.concatenate(decoded, axis=1)
    my_pos_user = jnp.where(decoded[4] < rows, decoded[5], -1)
    request, side_rows = lax.optimization_barrier((request.reshape(shards, 1, -1), side_rows))
    asked = lax.all_to_all(request, AXES, split_axis=0, concat_axis=0, tiled=True)
    moved, asked, w_two = exchange([(side_rows, side_order[1])], shards, [asked, w_two])
    side_rows = jnp.concatenate([side_rows, moved])
    asked = asked.reshape(shards, -1)
    for b in side_order[2:-2]:
        (moved,) = exchange([(side_rows, b)], shards)
        side_rows = jnp.concatenate([side_rows, moved])
    pos_row = asked[:, 4 * cap : 4 * cap + cap_pos]
    pos_user = asked[:, 4 * cap + cap_pos :]

    def prepared(start):
        row = asked[:, start : start + cap]
        user = asked[:, start + cap : start + 2 * cap]
        counts = jnp.sum((row < rows).astype(I32), axis=1)
        packed = 2 * row * (1 << SHIFT) + 2 * user
        packed = jnp.pad(packed, ((0, 0), (0, cap_pad - cap)), constant_values=2 * rows << SHIFT)
        return counts, packed.reshape(-1)

    watch_plan, search_plan = prepared(0), prepared(2 * cap)

    neg_count = shard_counts(neg_owner, shards)
    neg_most = jnp.max(neg_count)
    side_half = side_rows.shape[0] // 2
    side_parts = side_rows[:side_half], side_rows[side_half:]
    watch_counts, first_part = lax.optimization_barrier((watch_plan[0], side_parts[0]))
    send, watch_keep = pool(place_a, users, cap_pad, me, watch_counts, watch_plan[1], watch_table)
    first_got, send, watch_keep = exchange([(first_part, side_order[-2])], shards, [send, watch_keep])
    send, search_counts, second_part = lax.optimization_barrier((send, search_plan[0], side_parts[1]))
    search_send, search_keep = pool(place_b, users, cap_pad, me, search_counts, search_plan[1], search_table)
    watch_got, second_got, search_send, search_keep = exchange(
        [(send, order_a[0]), (second_part, side_order[-2])], shards, [search_send, search_keep]
    )
    side_rows = jnp.concatenate([side_rows, first_got, second_got])

    def cut(keep, got):
        half = keep.shape[0] // 2
        return keep[:half] + got[:half], keep[half:] + got[half:]

    (search_got,) = exchange([(search_send, order_b[0])], shards)
    for i in range(1, bits):
        watch_keep, watch_move = cut(watch_keep, watch_got)
        search_keep, search_move = cut(search_keep, search_got)
        moves = [(watch_move, order_a[i]), (search_move, order_b[i])]
        if i == 1:
            watch_move, search_move, side_rows = lax.optimization_barrier((watch_move, search_move, side_rows))
            served = out_table[jnp.minimum(pos_row, rows - 1)]
            fetched = lax.all_to_all(served, AXES, split_axis=0, concat_axis=0, tiled=True)
            side_got = swap(side_rows, 1 << side_order[-1], shards)
            watch_got, search_got, fetched, side_got = exchange(
                [(watch_move, order_a[i]), (search_move, order_b[i])], shards, [fetched, side_got]
            )
        else:
            watch_got, search_got = exchange(moves, shards)
    fetched = fetched.reshape(-1, width)
    watch_sum = watch_keep + watch_got
    search_sum = search_keep + search_got

    neg_rows = jnp.concatenate([side_rows, side_got])
    n_all = neg_rows.shape[0]
    gathered = neg_rows.reshape(-1, payload.shape[0], width)
    neg_count = shard_counts(neg_owner, shards)
    neg_most = jnp.max(neg_count)
    side_count = neg_count[mine ^ side_places]
    neg_real = jnp.arange(block, dtype=I32)[None, :] < side_count[:, None]
    neg_logq = gathered[:, block:, :].reshape(gathered.shape[0], -1)[:, :block]
    neg_logq = jnp.where(neg_real, neg_logq, BIG)
    neg_logq = jnp.pad(neg_logq, ((0, 0), (0, logq_rows)), constant_values=BIG).reshape(-1)

    watch_sum = watch_sum.reshape(users, width)
    search_sum = search_sum.reshape(users, width)
    watch_scale = 1.0 / watch_len.astype(F32)[:, None]
    search_scale = search_mask.astype(F32)[:, None] / search_len.astype(F32)[:, None]
    feats = jnp.concatenate([watch_sum * watch_scale, search_sum * search_scale, dense_feats], axis=1)

    def first_layer(x):
        return matmul(jnp.pad(x, ((0, 0), (0, bias_pad))), w_one) + b_one


    pos_match = my_pos_user.reshape(-1)[None, :] == user_index[:, None]
    pos_slot = jnp.sum(
        jnp.where(pos_match, jnp.arange(shards * cap_pos, dtype=I32)[None, :], 0), axis=1
    )
    pos_rows = fetched[pos_slot]

    neg_half = -(-negs // 2)
    assert neg_half <= n_all

    def all_negatives(state):
        local = jnp.where(neg_mine[:, None], out_table[neg_local], 0.0)
        full = jnp.pad(lax.psum(local, AXES), ((0, 2 * neg_half - negs), (0, 0)))
        logq = jnp.pad(logq_neg, (0, 2 * neg_half - negs), constant_values=BIG)
        return (
            jnp.zeros((), I32),
            jnp.pad(lax.dynamic_slice_in_dim(full, side * neg_half, neg_half), ((0, n_all - neg_half), (0, 0))),
            jnp.pad(
                lax.dynamic_slice_in_dim(logq, side * neg_half, neg_half), (0, n_all - neg_half), constant_values=BIG
            ),
        )

    overflow = (neg_most > block).astype(I32)
    _, neg_rows, neg_logq = lax.while_loop(
        lambda state: state[0] > 0, all_negatives, (overflow, neg_rows, neg_logq)
    )

    hidden_a, gelu_one = jax.vjp(jax.nn.gelu, first_layer(feats))
    hidden_b, gelu_two = jax.vjp(jax.nn.gelu, matmul(hidden_a, w_two) + b_two)
    user_vec, gelu_three = jax.vjp(jax.nn.gelu, matmul(hidden_b, weight_three) + bias_three)

    def side_sums(vectors):
        score = matmul_t(vectors, neg_rows) - neg_logq[None, :]
        top = jnp.max(score, axis=1)
        weight = jnp.exp(score - top[:, None])
        return matmul(weight, neg_rows), top, jnp.sum(weight, axis=1)

    partner_vec = swap(user_vec, 1 << side_bit, shards)
    g_here, top_here, sum_here = side_sums(user_vec)
    g_sent, top_sent, sum_sent = side_sums(partner_vec)
    sent = jnp.concatenate(
        [g_sent, jnp.pad(jnp.concatenate([top_sent, sum_sent])[None, :], ((0, 7), (0, width - 2 * users)))]
    )
    got = swap(sent, 1 << side_bit, shards)
    g_there, top_there, sum_there = got[:users], got[users, :users], got[users, users : 2 * users]
    s_pos = jnp.sum(user_vec * pos_rows, axis=1) - logq_pos
    top = jnp.maximum(jnp.maximum(top_here, top_there), s_pos)
    scale_here, scale_there, e_pos = jnp.exp(top_here - top), jnp.exp(top_there - top), jnp.exp(s_pos - top)
    totals = sum_here * scale_here + sum_there * scale_there + e_pos
    lse = top + jnp.log(totals)
    coef = e_pos / totals - 1.0
    g_user = (
        g_here * (scale_here / totals)[:, None]
        + g_there * (scale_there / totals)[:, None]
        + coef[:, None] * pos_rows
    )
    loss_sum = jnp.sum(lse - s_pos)
    user_rows = jnp.concatenate(
        [user_vec, jnp.pad(jnp.concatenate([lse, coef])[None, :], ((0, 7), (0, width - 2 * users)))]
    )

    user_rows = lax.all_gather(user_rows, AXES, axis=0, tiled=False)

    (g_three,) = gelu_three(g_user)
    (g_two,) = gelu_two(matmul_t(g_three, weight_three))
    (g_one,) = gelu_one(matmul_t(g_two, w_two))
    feats_held = after(feats, got)
    g_feats = matmul_t(g_one, w_one)[:, :n_feats]
    dense_grad = g_feats[:, 2 * width :]
    moved, g_feats = exchange([(feats_held, side_bit)], shards, [g_feats])
    feats_group = jnp.concatenate([feats, moved])
    group_order = [0, 1 << side_bit]

    watch_out = (g_feats[:, :width] * watch_scale).reshape(2 * users, LANES)
    search_out = (g_feats[:, width : 2 * width] * search_scale).reshape(2 * users, LANES)
    rows_three = weight_three.shape[0] // n_tp
    used_rows = weight_one.shape[0] + deep + rows_three + 4
    n_rows = -(-used_rows // (8 * n_dp)) * 8 * n_dp
    grads = jnp.stack(
        [
            jnp.concatenate(
                [
                    g_one[:, t * width : (t + 1) * width],
                    g_two[:, t * cols_two : (t + 1) * cols_two],
                    g_three,
                ],
                axis=1,
            )
            for t in range(n_tp)
        ]
    )
    dp_order = [*range(tp_bits + 1, bits), tp_bits]

    def halves(total, b):
        bit = (mine >> b) & 1
        half = total.shape[0] // 2
        return (
            lax.dynamic_slice_in_dim(total, bit * half, half, 0),
            lax.dynamic_slice_in_dim(total, (1 - bit) * half, half, 0),
        )

    def joined(total, other, b):
        bit = (mine >> b) & 1
        return jnp.concatenate([jnp.where(bit == 0, total, other), jnp.where(bit == 0, other, total)])

    watch_out, search_out, grads, feats_group = lax.optimization_barrier((watch_out, search_out, grads, feats_group))
    watch_pieces, search_pieces = [watch_out], [search_out]
    done = 0

    def scatter(total, b):
        kept, moved = halves(total, b)
        return kept, (moved, b)

    for i in reversed(range(1, bits)):
        watch_out, search_out = jnp.concatenate(watch_pieces), jnp.concatenate(search_pieces)
        moves = [(watch_out, order_a[i]), (search_out, order_b[i])]
        if i == bits - 1:
            grads = lax.all_to_all(grads, "tp", split_axis=0, concat_axis=0, tiled=True)
            for b in reversed(range(side_bit)):
                (moved,) = exchange([(feats_group, b)], shards)
                feats_group = jnp.concatenate([feats_group, moved])
                group_order = group_order + [r | 1 << b for r in group_order]
            feats_rest = feats_group[users:]
            a_rest = jax.nn.gelu(first_layer(feats_rest))
            b_rest = jax.nn.gelu(matmul(a_rest, w_two) + b_two)
            watch_got, search_got, a_rest, b_rest = exchange(moves, shards, [a_rest, b_rest])
        elif i == bits - 2:
            watch_got, search_got, grads = exchange(moves, shards, [grads])
            total = weight_block(
                group_order, n_rows, width, tp.astype(I32).reshape(1), loss_sum.reshape(1),
                feats, feats_rest, hidden_a, a_rest, hidden_b, b_rest, grads,
            )
            kept, move = scatter(total, dp_order[0])
            done = 1
        elif i > 1:
            watch_got, search_got, got = exchange(moves + [move], shards)
            kept, move = scatter(kept + got, dp_order[done])
            done += 1
        else:
            watch_out, search_out, first, user_rows = lax.optimization_barrier((watch_out, search_out, move[0], user_rows))
            output_grad = output_rows(
                users, block, cap_pos, jnp.sum(neg_mine.astype(I32)).reshape(1), own_rows_id, own_place, logq_neg,
                pos_row.reshape(-1), pos_user.reshape(-1), user_rows, out_table,
            )
            got, output_grad = exchange([(first, move[1])], shards, [output_grad])
            total = kept + got
            for b in dp_order[done:]:
                kept, move = scatter(total, b)
                (got,) = exchange([move], shards)
                total = kept + got
            watch_got, search_got, total = exchange(
                [(watch_out, order_a[i]), (search_out, order_b[i])], shards, [total]
            )
        watch_pieces, search_pieces = [watch_out, watch_got], [search_out, search_got]

    *far, got = exchange(
        [(x, order_a[0]) for x in watch_pieces] + [(x, order_b[0]) for x in search_pieces] + [(total, dp_order[-1])],
        shards,
    )
    total = joined(total, got, dp_order[-1])
    for b in reversed(dp_order[2:-1]):
        (got,) = exchange([(total, b)], shards)
        total = joined(total, got, b)
    watch_counts, total = lax.optimization_barrier((watch_plan[0], total))
    watch_grad = spread(place_a, users, cap_pad, rows, me, watch_counts, watch_plan[1], *watch_pieces, *far[:2])
    got, watch_grad = exchange([(total, dp_order[1])], shards, [watch_grad])
    total = joined(total, got, dp_order[1])
    search_counts, total = lax.optimization_barrier((search_plan[0], total))
    search_grad = spread(place_b, users, cap_pad, rows, me, search_counts, search_plan[1], *search_pieces, *far[2:])
    got, search_grad = exchange([(total, dp_order[0])], shards, [search_grad])
    total = joined(total, got, dp_order[0])

    at = weight_one.shape[0]
    w_one_grad = total[:at]
    w_two_grad = jnp.concatenate([total[at : at + deep, :cols_two], total[at : at + deep, cols_two:]])
    at += deep
    b_one_grad = total[at + rows_three]
    b_two_grad = total[at + rows_three + 1, :cols_two]
    b_three_grad = total[at + rows_three + 2]
    whole = total[at : at + rows_three + 8]
    others = exchange([(whole, *[b for b in range(tp_bits) if r >> b & 1]) for r in range(1, n_tp)], shards)
    whole = jnp.stack([whole, *others])
    whole = jnp.concatenate([lax.dynamic_slice_in_dim(whole, t ^ tp, 1, 0) for t in range(n_tp)])
    w_three_grad = whole[:, :rows_three].reshape(-1, width)
    mean_loss = jnp.sum(whole[:, rows_three + 3, 0]) / F32(users * shards)
    return (
        mean_loss,
        watch_grad,
        search_grad,
        output_grad,
        w_one_grad,
        b_one_grad,
        w_two_grad,
        b_two_grad,
        w_three_grad,
        b_three_grad,
        dense_grad,
    )


def solution(mesh):
    both = P(AXES)
    rows = P(AXES, None)
    in_specs = (
        rows, both, rows, both, both, both, both, P(), P(), rows, rows, rows, rows,
        P(None, "tp"), P("tp"), P(None, "tp"), P("tp"), P(), P(),
    )
    out_specs = (
        P(), rows, rows, rows, P(None, "tp"), P("tp"), P(None, "tp"), P("tp"), P(), P(), rows,
    )
    return jax.shard_map(body, mesh=mesh, in_specs=in_specs, out_specs=out_specs, check_vma=False)
```

time: 536 us -> 398 us (0.74)
  local copies, waits for them, and re-layouts: 141 us -> 44.8 us
  blocking collectives: 75.2 us -> 0 us
  waiting for transfers between devices: 70.2 us -> 121 us
  other arithmetic: 73.3 us -> 57.1 us
  starting transfers between devices: 37 us -> 52.2 us
  matrix products: 40.2 us -> 28.5 us
    all_gather x4 -> x0, blocking collectives: 75.2 us -> none  [the longest x1 58.2 us: body(): stats = lax.all_gather(jnp.stack([lse, coef]), AXES, axis=0, tiled=False)]
    gather x131 -> x3, local copies, waits for them, and re-layouts: 74.6 us -> 6.44 us  [the longest x1 3.08 us: body(): out_table[jnp.minimum(first_id, rows - 1)]]
    concatenate x8 -> x1, local copies, waits for them, and re-layouts: 26.6 us -> 2.8 us  [body(): neg_rows = jnp.concatenate([side_rows, side_got])]
    ppermute x28 -> x40, waiting for transfers between devices: 68.4 us -> 88.4 us  [swap(): return lax.ppermute(x, AXES, [(i, i ^ mask) for i in range(shards)])]
    all_gather x1, waiting for transfers between devices: 0.02 us -> 15.9 us  [body(): w_two = lax.all_gather(weight_two, 'tp', axis=1, tiled=True)]
    ppermute x28 -> x40, starting transfers between devices: 22.7 us -> 38.5 us  [swap(): return lax.ppermute(x, AXES, [(i, i ^ mask) for i in range(shards)])]
    all_to_all x1, waiting for transfers between devices: 0.01 us -> 15.6 us  [body(): lax.all_to_all(served, AXES, split_axis=0, concat_axis=0, tiled=True)]
    dot_general x12 -> x0, matrix products: 12.7 us -> none  [inner_rows(): lax.dot_general(left, right, (((0,), (0,)), ((), ())), precision=lax.Prec...]
  transfers between devices with their start and end apart: 34 -> 46, of which waited for: 13 -> 24; matrix products, arithmetic and copies ran while one was open for 47% -> 22% of each run, Pallas kernels for 13% -> 18%
where the time goes in v2:
time: 398 us; the launch traced here: 391 us
  waiting for transfers between devices  121 us (30%)
  Pallas kernels  70.1 us (18%)
  other arithmetic  57.1 us (14%)
  starting transfers between devices  52.2 us (13%)
  local copies, waits for them, and re-layouts  44.8 us (11%)
  matrix products  28.5 us (7%)
  between operations  18 us (5%)
    ppermute x40, waiting for transfers between devices, swap(): return lax.ppermute(x, AXES, [(i, i ^ mask) for i in range(shards)])  88.4 us
    ppermute x40, starting transfers between devices, swap(): return lax.ppermute(x, AXES, [(i, i ^ mask) for i in range(shards)])  38.5 us
    pallas_call x2, Pallas kernels, spread(): pl.pallas_call(functools.partial(spread_kernel, places, users, cap), out_...  28.7 us
    unnamed x138, local copies, waits for them, and re-layouts  20.8 us
    pallas_call x2, Pallas kernels, pool(): pl.pallas_call(functools.partial(pool_kernel, places, users, cap), out_sh...  19.8 us
    pallas_call x1, Pallas kernels, output_rows(): pl.pallas_call(functools.partial(output_kernel, users, block, cap_pos), o...  18.3 us
    dot_general x7, matrix products, matmul(): jnp.dot(left, right, precision=lax.Precision.HIGH, preferred_element_type...  17.1 us
    all_gather x1, waiting for transfers between devices, body(): w_two = lax.all_gather(weight_two, 'tp', axis=1, tiled=True)  15.9 us
  transfers between devices with their start and end apart: 46, of which 24 were waited for; matrix products, arithmetic and copies ran while one was open for 22% of the time, Pallas kernels for 18%

profile of v2, /device:TPU:0, one launch (start us, length us, event | category | flops | bytes accessed | tf_op | source)
XLA Modules:
  0.0 391.5 jit_solution(16268996239866748192)
XLA Ops:
  12.8 6.6 %sort.28 = (s32[5000]{0:T(1024)S(1)}, s32[5000]{0:T(1024)}) sort(s32[5000]{0:T(1024)S(1)} %get-tuple-element.412, s32[5000]{0:T(1024)S(1)} %iota.82), dimensions={0}, to_apply=%region_9.10 | sort | flops 65000 | bytes 80000 | tf_op jit(solution)/shard_map/sort | solution.py:409
  19.5 2.2 gather_fusion.2
  23.8 3.1 gather_fusion.1
  27.2 4.1 %collective-permute-start = (f32[216,256]{1,0:T(8,128)S(1)}, f32[216,256]{1,0:T(8,128)S(1)}, u32[]{:S(2)}, u32[]{:S(2)}) collective-permute-start(f32[216,256]{1,0:T(8,128)S(1)} %pad_maximum_fusion.24), channel_id=1, source_target_pairs={{0,16},{1,17},{2,18},{3,19},{4,20},{5,21},{6,22},{7,23},{8,24},{9,... | collective-permute-start | bytes 663560 | tf_op jit(solution)/shard_map/ppermute | solution.py:40
  31.4 11.2 %sort.29 = (s32[19392]{0:T(1024)S(1)}, s32[19392]{0:T(1024)}) sort(s32[19392]{0:T(1024)S(1)} %constant_dynamic-update-slice_fusion.2, s32[19392]{0:T(1024)S(1)} %iota.83), dimensions={0}, to_apply=%region_10.11 | sort | flops 290880 | bytes 310272 | tf_op jit(solution)/shard_map/sort | solution.py:448
  46.0 3.7 all-to-all-start
  49.7 15.9 %all-gather.7.cloned.1.call-done = f32[1024,512]{1,0:T(8,128)} async-done(((f32[1024,128]{1,0:T(8,128)}), f32[1024,512]{1,0:T(8,128)}) %all-gather.7.cloned.1.call-update) | async-done | bytes 2097168 | tf_op jit(solution)/shard_map/all_gather | solution.py:433
  67.5 2.2 copy-done.4
  69.7 11.6 %shard_map.287 = (f32[4096,128]{1,0:T(8,128)}, f32[4096,128]{1,0:T(8,128)S(1)}) custom-call(s32[1]{0:T(128)} %bitcast.5.me_ref, s32[32]{0:T(128)S(1)} %get-tuple-element.257.cnt_ref, s32[9728]{0:T(1024)S(1)} %reshape.264.idx_ref, f32[4096,256]{1,0:T(8,128)S(1)} %copy-done.4), custom_call_target="tpu_custom_call" | custom-call | bytes 41943040 | tf_op jit(solution)/shard_map/pallas_call | solution.py:108
  81.5 2.2 copy-done.5
  83.7 8.2 %shard_map.288 = (f32[4096,128]{1,0:T(8,128)S(1)}, f32[4096,128]{1,0:T(8,128)S(1)}) custom-call(s32[1]{0:T(128)} %bitcast.5.me_ref, s32[32]{0:T(128)S(1)} %get-tuple-element.262.cnt_ref, s32[9728]{0:T(1024)S(1)} %reshape.265.idx_ref, f32[4096,256]{1,0:T(8,128)S(1)} %copy-done.5), custom_call_target="tpu_custom_call" | custom-call | bytes 41943040 | tf_op jit(solution)/shard_map/pallas_call | solution.py:108
  91.9 2.3 collective-permute-done.4
  94.2 2.6 pad_maximum_fusion
  96.8 3.1 slice_add_fusion.2
  106.8 3.1 gather_fusion.3
  110.6 5.8 %all-to-all-start.1 = ((f32[32,6,256]{2,1,0:T(8,128)}), f32[32,6,256]{2,1,0:T(8,128)S(1)}, u32[]{:S(2)}, u32[]{:S(2)}) async-start(f32[32,6,256]{2,1,0:T(8,128)} %reshape.306), calls=%async_computation.1 | async-start | bytes 524288 | tf_op jit(solution)/shard_map/all_to_all | solution.py:508
  117.3 15.6 %all-to-all-done.1 = f32[32,6,256]{2,1,0:T(8,128)S(1)} async-done(((f32[32,6,256]{2,1,0:T(8,128)}), f32[32,6,256]{2,1,0:T(8,128)S(1)}, u32[]{:S(2)}, u32[]{:S(2)}) %all-to-all-start.1) | async-done | bytes 196640 | tf_op jit(solution)/shard_map/all_to_all | solution.py:508
  138.7 2.8 constant_dynamic-update-slice_fusion.1
  141.5 9.7 %collective-permute-done.9 = f32[1024,128]{1,0:T(8,128)S(1)} collective-permute-done((f32[1024,128]{1,0:T(8,128)}, f32[1024,128]{1,0:T(8,128)S(1)}, u32[]{:S(2)}, u32[]{:S(2)}) %collective-permute-start.9) | collective-permute-done | bytes 524320 | tf_op jit(solution)/shard_map/ppermute | solution.py:40
  155.3 2.8 constant_dynamic-update-slice_fusion
  159.1 3.4 collective-permute-done.11
  162.5 3.8 collective-permute-done.12
  170.9 7.1 %collective-permute-done.13 = f32[256,128]{1,0:T(8,128)S(1)} collective-permute-done((f32[256,128]{1,0:T(8,128)S(1)}, f32[256,128]{1,0:T(8,128)S(1)}, u32[]{:S(2)}, u32[]{:S(2)}) %collective-permute-start.13) | collective-permute-done | bytes 131104 | tf_op jit(solution)/shard_map/ppermute | solution.py:40
  180.8 2.8 convolution_add_fusion.1
  188.8 4.0 %fusion.96 = (f32[128]{0:T(128)S(1)}, f32[128,3456]{1,0:T(8,128)S(1)}) fusion(f32[3456]{0:T(1024)} %get-tuple-element.214, f32[3456,256]{1,0:T(8,128)} %get-tuple-element.213, f32[128,256]{1,0:T(8,128)S(1)} %get-tuple-element.423), kind=kOutput, calls=%fused_computation.316 | convolution fusion | flops 680624000 | bytes 5453824 | tf_op jit(solution)/shard_map/dot_general | solution.py:28
  192.9 3.0 fusion.95
  199.0 3.9 collective-permute-done.16
  206.0 3.8 fusion.45
  219.1 3.7 all-to-all-start.2
  223.0 2.9 collective-permute-start.19
  226.0 4.4 %fusion.6.refs_3_ = f32[384,1024]{1,0:T(8,128)S(1)} fusion(f32[648,1024]{1,0:T(8,128)} %all-gather.5.cloned.1.call-done, f32[384,640]{1,0:T(8,128)S(1)} %pad_maximum_fusion.4.refs_1_, f32[1024]{0:T(1024)S(1)} %bitcast.95), kind=kOutput, calls=%fused_computation.21 | convolution fusion | flops 1532362752 | bytes 5214208 | tf_op jit(solution)/shard_map/dot_general | solution.py:24
  230.4 2.7 fusion.21.refs_5_
  233.1 5.1 %collective-permute-done.18 = f32[256,128]{1,0:T(8,128)S(1)} collective-permute-done((f32[256,128]{1,0:T(8,128)}, f32[256,128]{1,0:T(8,128)S(1)}, u32[]{:S(2)}, u32[]{:S(2)}) %collective-permute-start.18) | collective-permute-done | bytes 131104 | tf_op jit(solution)/shard_map/ppermute | solution.py:40
  238.2 3.3 collective-permute-done.19
  246.9 7.5 %collective-permute-done.21 = f32[512,128]{1,0:T(8,128)} collective-permute-done((f32[512,128]{1,0:T(8,128)}, f32[512,128]{1,0:T(8,128)}, u32[]{:S(2)}, u32[]{:S(2)}) %collective-permute-start.21) | collective-permute-done | bytes 262176 | tf_op jit(solution)/shard_map/ppermute | solution.py:40
  254.4 13.8 %collective-permute-done.22 = f32[512,128]{1,0:T(8,128)} collective-permute-done((f32[512,128]{1,0:T(8,128)}, f32[512,128]{1,0:T(8,128)}, u32[]{:S(2)}, u32[]{:S(2)}) %collective-permute-start.22) | collective-permute-done | bytes 262176 | tf_op jit(solution)/shard_map/ppermute | solution.py:40
  276.0 3.4 shard_map.289
  283.3 2.5 collective-permute-start.24
  285.8 7.0 %collective-permute-done.23 = f32[1024,128]{1,0:T(8,128)} collective-permute-done((f32[1024,128]{1,0:T(8,128)}, f32[1024,128]{1,0:T(8,128)}, u32[]{:S(2)}, u32[]{:S(2)}) %collective-permute-start.23) | collective-permute-done | bytes 524320 | tf_op jit(solution)/shard_map/ppermute | solution.py:40
  299.6 2.5 collective-permute-start.26
  302.9 2.3 copy-done.3
  305.2 18.3 %shard_map.290 = f32[4096,256]{1,0:T(8,128)} custom-call(s32[1]{0:T(128)} %bitcast.22.cnt_ref, s32[5208]{0:T(1024)S(1)} %pad.63.id_ref, s32[5208]{0:T(1024)S(1)} %pad.64.place_ref, f32[5000]{0:T(1024)S(1)} %copy-done.19, s32[192]{0:T(256)S(1)} %reshape.278.pos_ref, s32[192]{0:T(256)S(1)} %reshape.279.pos_user_ref, f32[32,136,256]{2,1,0:T(8,128)S(1)} %bitcast.81, ...), custom_call_target="tpu_custom_call" | custom-call | bytes 41943040 | tf_op jit(solution)/shard_map/pallas_call | solution.py:319
  325.2 3.9 collective-permute-done.29
  331.8 4.8 %collective-permute-done.34 = f32[168,256]{1,0:T(8,128)S(1)} collective-permute-done((f32[168,256]{1,0:T(8,128)S(1)}, f32[168,256]{1,0:T(8,128)S(1)}, u32[]{:S(2)}, u32[]{:S(2)}) %collective-permute-start.34) | collective-permute-done | bytes 172064 | tf_op jit(solution)/shard_map/ppermute | solution.py:40
  338.1 15.8 %shard_map.291 = f32[4096,256]{1,0:T(8,128)} custom-call(s32[1]{0:T(128)} %bitcast.5.me_ref, s32[32]{0:T(128)S(1)} %copy-done.16, s32[9728]{0:T(1024)S(1)} %reshape.264.idx_ref, f32[2048,128]{1,0:T(8,128)S(1)} %pad_maximum_fusion.2.refs_0_, f32[2048,128]{1,0:T(8,128)} %collective-permute-done.26.refs_1_, f32[2048,128]{1,0:T(8,128)} %collective-permute-done.30.refs_2_, ...), custom_call_target="tpu_custom_call" | custom-call | bytes 41943040 | tf_op jit(solution)/shard_map/pallas_call | solution.py:159
  356.2 12.9 %shard_map.292 = f32[4096,256]{1,0:T(8,128)} custom-call(s32[1]{0:T(128)} %bitcast.5.me_ref, s32[32]{0:T(128)S(1)} %copy-done.14, s32[9728]{0:T(1024)S(1)} %reshape.265.idx_ref, f32[2048,128]{1,0:T(8,128)S(1)} %pad_maximum_fusion.3.refs_0_, f32[2048,128]{1,0:T(8,128)} %collective-permute-done.27.refs_1_, f32[2048,128]{1,0:T(8,128)} %collective-permute-done.32.refs_2_, ...), custom_call_target="tpu_custom_call" | custom-call | bytes 41943040 | tf_op jit(solution)/shard_map/pallas_call | solution.py:159
  369.1 3.0 collective-permute-done.36
  376.9 2.5 collective-permute-done.38
  (355 shorter events, 100.6 us)
Async XLA Ops:
  7.2 178.9 %copy-start = (f32[512,256]{1,0:T(8,128)S(1)}, f32[512,256]{1,0:T(8,128)}, u32[]{:S(2)}) copy-start(f32[512,256]{1,0:T(8,128)} %param.39) | copy-start | bytes 1572868
  7.2 35.5 %all-gather.5.cloned.1.call-start = ((), (), s32[]{:S(2)}) async-start(), calls=%async_computation.4 | async-start | bytes 3317760 | tf_op jit(solution)/shard_map/all_gather | solution.py:432
  10.7 54.8 %all-gather.7.cloned.1.call-start = ((), (), s32[]{:S(2)}) async-start(), calls=%async_computation.5 | async-start | bytes 2621440 | tf_op jit(solution)/shard_map/all_gather | solution.py:433
  27.2 15.3 %collective-permute-start = (f32[216,256]{1,0:T(8,128)S(1)}, f32[216,256]{1,0:T(8,128)S(1)}, u32[]{:S(2)}, u32[]{:S(2)}) collective-permute-start(f32[216,256]{1,0:T(8,128)S(1)} %pad_maximum_fusion.24), channel_id=1, source_target_pairs={{0,16},{1,17},{2,18},{3,19},{4,20},{5,21},{6,22},{7,23},{8,24},{9,... | collective-permute-start | bytes 663560 | tf_op jit(solution)/shard_map/ppermute | solution.py:40
  43.5 22.1 %collective-permute-start.1 = (f32[432,256]{1,0:T(8,128)S(1)}, f32[432,256]{1,0:T(8,128)}, u32[]{:S(2)}, u32[]{:S(2)}) collective-permute-start(f32[432,256]{1,0:T(8,128)S(1)} %pad_maximum_fusion.19), channel_id=1, source_target_pairs={{0,8},{1,9},{2,10},{3,11},{4,12},{5,13},{6,14},{7,15},{8,0},{9,1},... | collective-permute-start | bytes 1327112 | tf_op jit(solution)/shard_map/ppermute | solution.py:40
  46.0 19.6 %all-to-all-start = ((s32[32,1,1212]{2,1,0:T(1,128)}), s32[32,1,1212]{2,1,0:T(1,128)S(1)}, u32[]{:S(2)}, u32[]{:S(2)}) async-start(s32[32,1,1212]{2,1,0:T(1,128)} %copy.44), calls=%async_computation | async-start | bytes 327680 | tf_op jit(solution)/shard_map/all_to_all | solution.py:462
  65.8 15.4 %collective-permute-start.2 = (f32[432,256]{1,0:T(8,128)S(1)}, f32[432,256]{1,0:T(8,128)}, u32[]{:S(2)}, u32[]{:S(2)}) collective-permute-start(f32[432,256]{1,0:T(8,128)S(1)} %pad_maximum_fusion.19), channel_id=1, source_target_pairs={{0,4},{1,5},{2,6},{3,7},{4,0},{5,1},{6,2},{7,3},{8,12},{9,13},{10,... | collective-permute-start | bytes 1327112 | tf_op jit(solution)/shard_map/ppermute | solution.py:40
  81.3 13.0 %collective-permute-start.3 = (f32[4096,128]{1,0:T(8,128)}, f32[4096,128]{1,0:T(8,128)}, u32[]{:S(2)}, u32[]{:S(2)}) collective-permute-start(f32[4096,128]{1,0:T(8,128)} %get-tuple-element.181), channel_id=1, source_target_pairs={{0,1},{1,0},{2,3},{3,2},{4,5},{5,4},{6,7},{7,6},{8,9},{9,8},{10,11... | collective-permute-start | bytes 6291464 | tf_op jit(solution)/shard_map/ppermute | solution.py:40
  81.3 12.9 %collective-permute-start.4 = (f32[432,256]{1,0:T(8,128)}, f32[432,256]{1,0:T(8,128)}, u32[]{:S(2)}, u32[]{:S(2)}) collective-permute-start(f32[432,256]{1,0:T(8,128)} %collective-permute-done.1), channel_id=1, source_target_pairs={{0,4},{1,5},{2,6},{3,7},{4,0},{5,1},{6,2},{7,3},{8,12},{9,13},{10,... | collective-permute-start | bytes 1327112 | tf_op jit(solution)/shard_map/ppermute | solution.py:40
  94.2 5.8 %collective-permute-start.5 = (f32[4096,128]{1,0:T(8,128)S(1)}, f32[4096,128]{1,0:T(8,128)S(1)}, u32[]{:S(2)}, u32[]{:S(2)}) collective-permute-start(f32[4096,128]{1,0:T(8,128)S(1)} %get-tuple-element.188), channel_id=1, source_target_pairs={{0,1},{1,0},{2,3},{3,2},{4,5},{5,4},{6,7},{7,6},{8,9},{9,8},{10,11... | collective-permute-start | bytes 6291464 | tf_op jit(solution)/shard_map/ppermute | solution.py:40
  101.2 31.7 %copy-start.26 = (f32[2048,128]{1,0:T(8,128)S(1)}, f32[2048,128]{1,0:T(8,128)}, u32[]{:S(2)}) copy-start(f32[2048,128]{1,0:T(8,128)} %get-tuple-element.347) | copy-start | bytes 3145732
  101.2 31.7 %collective-permute-start.8 = (f32[1728,256]{1,0:T(8,128)}, f32[1728,256]{1,0:T(8,128)}, u32[]{:S(2)}, u32[]{:S(2)}) collective-permute-start(f32[1728,256]{1,0:T(8,128)} %pad_maximum_fusion), channel_id=1, source_target_pairs={{0,1},{1,0},{2,3},{3,2},{4,5},{5,4},{6,7},{7,6},{8,9},{9,8},{10,11... | collective-permute-start | bytes 5308424 | tf_op jit(solution)/shard_map/ppermute | solution.py:40
  104.4 28.5 %collective-permute-start.6 = (f32[2048,128]{1,0:T(8,128)}, f32[2048,128]{1,0:T(8,128)}, u32[]{:S(2)}, u32[]{:S(2)}) collective-permute-start(f32[2048,128]{1,0:T(8,128)} %get-tuple-element.193), channel_id=1, source_target_pairs={{0,2},{1,3},{2,0},{3,1},{4,6},{5,7},{6,4},{7,5},{8,10},{9,11},{10,... | collective-permute-start | bytes 3145736 | tf_op jit(solution)/shard_map/ppermute | solution.py:40
  105.1 27.8 %collective-permute-start.7 = (f32[2048,128]{1,0:T(8,128)}, f32[2048,128]{1,0:T(8,128)}, u32[]{:S(2)}, u32[]{:S(2)}) collective-permute-start(f32[2048,128]{1,0:T(8,128)} %get-tuple-element.194), channel_id=1, source_target_pairs={{0,4},{1,5},{2,6},{3,7},{4,0},{5,1},{6,2},{7,3},{8,12},{9,13},{10,... | collective-permute-start | bytes 3145736 | tf_op jit(solution)/shard_map/ppermute | solution.py:40
  110.6 22.3 %all-to-all-start.1 = ((f32[32,6,256]{2,1,0:T(8,128)}), f32[32,6,256]{2,1,0:T(8,128)S(1)}, u32[]{:S(2)}, u32[]{:S(2)}) async-start(f32[32,6,256]{2,1,0:T(8,128)} %reshape.306), calls=%async_computation.1 | async-start | bytes 524288 | tf_op jit(solution)/shard_map/all_to_all | solution.py:508
  137.1 14.1 %collective-permute-start.9 = (f32[1024,128]{1,0:T(8,128)}, f32[1024,128]{1,0:T(8,128)S(1)}, u32[]{:S(2)}, u32[]{:S(2)}) collective-permute-start(f32[1024,128]{1,0:T(8,128)} %get-tuple-element.198), channel_id=1, source_target_pairs={{0,4},{1,5},{2,6},{3,7},{4,0},{5,1},{6,2},{7,3},{8,12},{9,13},{10,... | collective-permute-start | bytes 1572872 | tf_op jit(solution)/shard_map/ppermute | solution.py:40
  138.0 13.9 %collective-permute-start.10 = (f32[1024,128]{1,0:T(8,128)}, f32[1024,128]{1,0:T(8,128)S(1)}, u32[]{:S(2)}, u32[]{:S(2)}) collective-permute-start(f32[1024,128]{1,0:T(8,128)} %get-tuple-element.199), channel_id=1, source_target_pairs={{0,2},{1,3},{2,0},{3,1},{4,6},{5,7},{6,4},{7,5},{8,10},{9,11},{10,... | collective-permute-start | bytes 1572872 | tf_op jit(solution)/shard_map/ppermute | solution.py:40
  153.2 9.3 %collective-permute-start.11 = (f32[512,128]{1,0:T(8,128)S(1)}, f32[512,128]{1,0:T(8,128)S(1)}, u32[]{:S(2)}, u32[]{:S(2)}) collective-permute-start(f32[512,128]{1,0:T(8,128)S(1)} %get-tuple-element.202), channel_id=1, source_target_pairs={{0,8},{1,9},{2,10},{3,11},{4,12},{5,13},{6,14},{7,15},{8,0},{9,1},... | collective-permute-start | bytes 786440 | tf_op jit(solution)/shard_map/ppermute | solution.py:40
  154.4 11.9 %collective-permute-start.12 = (f32[512,128]{1,0:T(8,128)S(1)}, f32[512,128]{1,0:T(8,128)S(1)}, u32[]{:S(2)}, u32[]{:S(2)}) collective-permute-start(f32[512,128]{1,0:T(8,128)S(1)} %get-tuple-element.203), channel_id=1, source_target_pairs={{0,8},{1,9},{2,10},{3,11},{4,12},{5,13},{6,14},{7,15},{8,0},{9,1},... | collective-permute-start | bytes 786440 | tf_op jit(solution)/shard_map/ppermute | solution.py:40
  166.3 11.6 %collective-permute-start.13 = (f32[256,128]{1,0:T(8,128)S(1)}, f32[256,128]{1,0:T(8,128)S(1)}, u32[]{:S(2)}, u32[]{:S(2)}) collective-permute-start(f32[256,128]{1,0:T(8,128)S(1)} %slice_add_fusion.14), channel_id=1, source_target_pairs={{0,16},{1,17},{2,18},{3,19},{4,20},{5,21},{6,22},{7,23},{8,24},{9,... | collective-permute-start | bytes 393224 | tf_op jit(solution)/shard_map/ppermute | solution.py:40
  168.4 11.0 %collective-permute-start.14 = (f32[256,128]{1,0:T(8,128)S(1)}, f32[256,128]{1,0:T(8,128)S(1)}, u32[]{:S(2)}, u32[]{:S(2)}) collective-permute-start(f32[256,128]{1,0:T(8,128)S(1)} %slice_add_fusion.13), channel_id=1, source_target_pairs={{0,16},{1,17},{2,18},{3,19},{4,20},{5,21},{6,22},{7,23},{8,24},{9,... | collective-permute-start | bytes 393224 | tf_op jit(solution)/shard_map/ppermute | solution.py:40
  187.1 5.8 %collective-permute-start.15 = (f32[128,256]{1,0:T(8,128)}, f32[128,256]{1,0:T(8,128)}, u32[]{:S(2)}, u32[]{:S(2)}) collective-permute-start(f32[128,256]{1,0:T(8,128)} %get-tuple-element.398), channel_id=1, source_target_pairs={{0,2},{1,3},{2,0},{3,1},{4,6},{5,7},{6,4},{7,5},{8,10},{9,11},{10,... | collective-permute-start | bytes 393224 | tf_op jit(solution)/shard_map/ppermute | solution.py:40
  188.4 109.5 %all-gather.9.cloned.1.call-start = ((), (), s32[]{:S(2)}) async-start(), calls=%async_computation.6 | async-start | bytes 4595712 | tf_op jit(solution)/shard_map/all_gather | solution.py:600
  197.7 5.1 %collective-permute-start.16 = (f32[136,256]{1,0:T(8,128)S(1)}, f32[136,256]{1,0:T(8,128)S(1)}, u32[]{:S(2)}, u32[]{:S(2)}) collective-permute-start(f32[136,256]{1,0:T(8,128)S(1)} %select_maximum_fusion.2), channel_id=1, source_target_pairs={{0,2},{1,3},{2,0},{3,1},{4,6},{5,7},{6,4},{7,5},{8,10},{9,11},{10,... | collective-permute-start | bytes 417800 | tf_op jit(solution)/shard_map/ppermute | solution.py:40
  205.2 11.5 %collective-permute-start.17 = (f32[128,640]{1,0:T(8,128)S(1)}, f32[128,640]{1,0:T(8,128)}, u32[]{:S(2)}, u32[]{:S(2)}) collective-permute-start(f32[128,640]{1,0:T(8,128)S(1)} %pad_maximum_fusion.21.refs_0_), channel_id=1, source_target_pairs={{0,2},{1,3},{2,0},{3,1},{4,6},{5,7},{6,4},{7,5},{8,10},{9,11},{10,... | collective-permute-start | bytes 983048 | tf_op jit(solution)/shard_map/ppermute | solution.py:40
  219.1 6.8 %collective-permute-start.20 = (f32[256,640]{1,0:T(8,128)S(1)}, f32[256,640]{1,0:T(8,128)S(1)}, u32[]{:S(2)}, u32[]{:S(2)}) collective-permute-start(f32[256,640]{1,0:T(8,128)S(1)} %pad_maximum_fusion.7), channel_id=1, source_target_pairs={{0,1},{1,0},{2,3},{3,2},{4,5},{5,4},{6,7},{7,6},{8,9},{9,8},{10,11... | collective-permute-start | bytes 1966088 | tf_op jit(solution)/shard_map/ppermute | solution.py:40
  219.1 49.1 %all-to-all-start.2 = ((f32[4,128,640]{2,1,0:T(8,128)}), f32[4,128,640]{2,1,0:T(8,128)S(1)}, u32[]{:S(2)}, u32[]{:S(2)}) async-start(f32[4,128,640]{2,1,0:T(8,128)} %pad_maximum_fusion.1), calls=%async_computation.2 | async-start | bytes 2621440 | tf_op jit(solution)/shard_map/all_to_all | solution.py:656
  222.9 15.3 %collective-permute-start.18 = (f32[256,128]{1,0:T(8,128)}, f32[256,128]{1,0:T(8,128)S(1)}, u32[]{:S(2)}, u32[]{:S(2)}) collective-permute-start(f32[256,128]{1,0:T(8,128)} %reshape.273), channel_id=1, source_target_pairs={{0,16},{1,17},{2,18},{3,19},{4,20},{5,21},{6,22},{7,23},{8,24},{9,... | collective-permute-start | bytes 393224 | tf_op jit(solution)/shard_map/ppermute | solution.py:40
  223.0 18.6 %collective-permute-start.19 = (f32[256,128]{1,0:T(8,128)}, f32[256,128]{1,0:T(8,128)S(1)}, u32[]{:S(2)}, u32[]{:S(2)}) collective-permute-start(f32[256,128]{1,0:T(8,128)} %reshape.274), channel_id=1, source_target_pairs={{0,16},{1,17},{2,18},{3,19},{4,20},{5,21},{6,22},{7,23},{8,24},{9,... | collective-permute-start | bytes 393224 | tf_op jit(solution)/shard_map/ppermute | solution.py:40
  244.9 9.6 %collective-permute-start.21 = (f32[512,128]{1,0:T(8,128)}, f32[512,128]{1,0:T(8,128)}, u32[]{:S(2)}, u32[]{:S(2)}) collective-permute-start(f32[512,128]{1,0:T(8,128)} %pad_maximum_fusion.22), channel_id=1, source_target_pairs={{0,8},{1,9},{2,10},{3,11},{4,12},{5,13},{6,14},{7,15},{8,0},{9,1},... | collective-permute-start | bytes 786440 | tf_op jit(solution)/shard_map/ppermute | solution.py:40
  244.9 23.4 %collective-permute-start.22 = (f32[512,128]{1,0:T(8,128)}, f32[512,128]{1,0:T(8,128)}, u32[]{:S(2)}, u32[]{:S(2)}) collective-permute-start(f32[512,128]{1,0:T(8,128)} %pad_maximum_fusion.23), channel_id=1, source_target_pairs={{0,8},{1,9},{2,10},{3,11},{4,12},{5,13},{6,14},{7,15},{8,0},{9,1},... | collective-permute-start | bytes 786440 | tf_op jit(solution)/shard_map/ppermute | solution.py:40
  283.1 11.2 %collective-permute-start.25 = (f32[672,256]{1,0:T(8,128)S(1)}, f32[672,256]{1,0:T(8,128)S(1)}, u32[]{:S(2)}, u32[]{:S(2)}) collective-permute-start(f32[672,256]{1,0:T(8,128)S(1)} %constant_dynamic-slice_fusion.5), channel_id=1, source_target_pairs={{0,8},{1,9},{2,10},{3,11},{4,12},{5,13},{6,14},{7,15},{8,0},{9,1},... | collective-permute-start | bytes 2064392 | tf_op jit(solution)/shard_map/ppermute | solution.py:40
  283.2 9.6 %collective-permute-start.23 = (f32[1024,128]{1,0:T(8,128)}, f32[1024,128]{1,0:T(8,128)}, u32[]{:S(2)}, u32[]{:S(2)}) collective-permute-start(f32[1024,128]{1,0:T(8,128)} %pad_maximum_fusion.17), channel_id=1, source_target_pairs={{0,4},{1,5},{2,6},{3,7},{4,0},{5,1},{6,2},{7,3},{8,12},{9,13},{10,... | collective-permute-start | bytes 1572872 | tf_op jit(solution)/shard_map/ppermute | solution.py:40
  283.3 10.0 %collective-permute-start.24 = (f32[1024,128]{1,0:T(8,128)}, f32[1024,128]{1,0:T(8,128)}, u32[]{:S(2)}, u32[]{:S(2)}) collective-permute-start(f32[1024,128]{1,0:T(8,128)} %pad_maximum_fusion.18), channel_id=1, source_target_pairs={{0,2},{1,3},{2,0},{3,1},{4,6},{5,7},{6,4},{7,5},{8,10},{9,11},{10,... | collective-permute-start | bytes 1572872 | tf_op jit(solution)/shard_map/ppermute | solution.py:40
  297.9 25.6 %collective-permute-start.28 = (f32[336,256]{1,0:T(8,128)}, f32[336,256]{1,0:T(8,128)S(1)}, u32[]{:S(2)}, u32[]{:S(2)}) collective-permute-start(f32[336,256]{1,0:T(8,128)} %constant_dynamic-slice_fusion.4), channel_id=1, source_target_pairs={{0,16},{1,17},{2,18},{3,19},{4,20},{5,21},{6,22},{7,23},{8,24},{9,... | collective-permute-start | bytes 1032200 | tf_op jit(solution)/shard_map/ppermute | solution.py:40
  299.6 29.5 %collective-permute-start.26 = (f32[2048,128]{1,0:T(8,128)S(1)}, f32[2048,128]{1,0:T(8,128)}, u32[]{:S(2)}, u32[]{:S(2)}) collective-permute-start(f32[2048,128]{1,0:T(8,128)S(1)} %pad_maximum_fusion.2.refs_0_), channel_id=1, source_target_pairs={{0,2},{1,3},{2,0},{3,1},{4,6},{5,7},{6,4},{7,5},{8,10},{9,11},{10,... | collective-permute-start | bytes 3145736 | tf_op jit(solution)/shard_map/ppermute | solution.py:40
  302.1 27.0 %collective-permute-start.27 = (f32[2048,128]{1,0:T(8,128)S(1)}, f32[2048,128]{1,0:T(8,128)}, u32[]{:S(2)}, u32[]{:S(2)}) collective-permute-start(f32[2048,128]{1,0:T(8,128)S(1)} %pad_maximum_fusion.3.refs_0_), channel_id=1, source_target_pairs={{0,4},{1,5},{2,6},{3,7},{4,0},{5,1},{6,2},{7,3},{8,12},{9,13},{10,... | collective-permute-start | bytes 3145736 | tf_op jit(solution)/shard_map/ppermute | solution.py:40
  323.6 5.5 %collective-permute-start.29 = (f32[168,256]{1,0:T(8,128)S(1)}, f32[168,256]{1,0:T(8,128)S(1)}, u32[]{:S(2)}, u32[]{:S(2)}) collective-permute-start(f32[168,256]{1,0:T(8,128)S(1)} %constant_dynamic-slice_fusion.3), channel_id=1, source_target_pairs={{0,4},{1,5},{2,6},{3,7},{4,0},{5,1},{6,2},{7,3},{8,12},{9,13},{10,... | collective-permute-start | bytes 516104 | tf_op jit(solution)/shard_map/ppermute | solution.py:40
  329.1 7.5 %collective-permute-start.30 = (f32[2048,128]{1,0:T(8,128)S(1)}, f32[2048,128]{1,0:T(8,128)}, u32[]{:S(2)}, u32[]{:S(2)}) collective-permute-start(f32[2048,128]{1,0:T(8,128)S(1)} %pad_maximum_fusion.2.refs_0_), channel_id=1, source_target_pairs={{0,1},{1,0},{2,3},{3,2},{4,5},{5,4},{6,7},{7,6},{8,9},{9,8},{10,11... | collective-permute-start | bytes 3145736 | tf_op jit(solution)/shard_map/ppermute | solution.py:40
  329.2 7.4 %collective-permute-start.31 = (f32[2048,128]{1,0:T(8,128)}, f32[2048,128]{1,0:T(8,128)}, u32[]{:S(2)}, u32[]{:S(2)}) collective-permute-start(f32[2048,128]{1,0:T(8,128)} %collective-permute-done.26.refs_1_), channel_id=1, source_target_pairs={{0,1},{1,0},{2,3},{3,2},{4,5},{5,4},{6,7},{7,6},{8,9},{9,8},{10,11... | collective-permute-start | bytes 3145736 | tf_op jit(solution)/shard_map/ppermute | solution.py:40
  329.7 6.9 %collective-permute-start.32 = (f32[2048,128]{1,0:T(8,128)S(1)}, f32[2048,128]{1,0:T(8,128)}, u32[]{:S(2)}, u32[]{:S(2)}) collective-permute-start(f32[2048,128]{1,0:T(8,128)S(1)} %pad_maximum_fusion.3.refs_0_), channel_id=1, source_target_pairs={{0,1},{1,0},{2,3},{3,2},{4,5},{5,4},{6,7},{7,6},{8,9},{9,8},{10,11... | collective-permute-start | bytes 3145736 | tf_op jit(solution)/shard_map/ppermute | solution.py:40
  329.8 6.9 %collective-permute-start.33 = (f32[2048,128]{1,0:T(8,128)}, f32[2048,128]{1,0:T(8,128)}, u32[]{:S(2)}, u32[]{:S(2)}) collective-permute-start(f32[2048,128]{1,0:T(8,128)} %collective-permute-done.27.refs_1_), channel_id=1, source_target_pairs={{0,1},{1,0},{2,3},{3,2},{4,5},{5,4},{6,7},{7,6},{8,9},{9,8},{10,11... | collective-permute-start | bytes 3145736 | tf_op jit(solution)/shard_map/ppermute | solution.py:40
  330.2 6.4 %collective-permute-start.34 = (f32[168,256]{1,0:T(8,128)S(1)}, f32[168,256]{1,0:T(8,128)S(1)}, u32[]{:S(2)}, u32[]{:S(2)}) collective-permute-start(f32[168,256]{1,0:T(8,128)S(1)} %dynamic-slice_add_fusion.2), channel_id=1, source_target_pairs={{0,4},{1,5},{2,6},{3,7},{4,0},{5,1},{6,2},{7,3},{8,12},{9,13},{10,... | collective-permute-start | bytes 516104 | tf_op jit(solution)/shard_map/ppermute | solution.py:40
  336.8 18.4 %collective-permute-start.35 = (f32[336,256]{1,0:T(8,128)S(1)}, f32[336,256]{1,0:T(8,128)S(1)}, u32[]{:S(2)}, u32[]{:S(2)}) collective-permute-start(f32[336,256]{1,0:T(8,128)S(1)} %pad_maximum_fusion.20), channel_id=1, source_target_pairs={{0,16},{1,17},{2,18},{3,19},{4,20},{5,21},{6,22},{7,23},{8,24},{9,... | collective-permute-start | bytes 1032200 | tf_op jit(solution)/shard_map/ppermute | solution.py:40
  355.3 16.7 %collective-permute-start.36 = (f32[672,256]{1,0:T(8,128)S(1)}, f32[672,256]{1,0:T(8,128)S(1)}, u32[]{:S(2)}, u32[]{:S(2)}) collective-permute-start(f32[672,256]{1,0:T(8,128)S(1)} %pad_maximum_fusion.5), channel_id=1, source_target_pairs={{0,8},{1,9},{2,10},{3,11},{4,12},{5,13},{6,14},{7,15},{8,0},{9,1},... | collective-permute-start | bytes 2064392 | tf_op jit(solution)/shard_map/ppermute | solution.py:40
  372.7 4.2 %collective-permute-start.37 = (f32[136,256]{1,0:T(8,128)S(1)}, f32[136,256]{1,0:T(8,128)S(1)}, u32[]{:S(2)}, u32[]{:S(2)}) collective-permute-start(f32[136,256]{1,0:T(8,128)S(1)} %get-tuple-element.268), channel_id=1, source_target_pairs={{0,1},{1,0},{2,3},{3,2},{4,5},{5,4},{6,7},{7,6},{8,9},{9,8},{10,11... | collective-permute-start | bytes 417800 | tf_op jit(solution)/shard_map/ppermute | solution.py:40
  372.8 6.5 %collective-permute-start.38 = (f32[136,256]{1,0:T(8,128)S(1)}, f32[136,256]{1,0:T(8,128)S(1)}, u32[]{:S(2)}, u32[]{:S(2)}) collective-permute-start(f32[136,256]{1,0:T(8,128)S(1)} %get-tuple-element.268), channel_id=1, source_target_pairs={{0,2},{1,3},{2,0},{3,1},{4,6},{5,7},{6,4},{7,5},{8,10},{9,11},{10,... | collective-permute-start | bytes 417800 | tf_op jit(solution)/shard_map/ppermute | solution.py:40
  372.9 8.5 %collective-permute-start.39 = (f32[136,256]{1,0:T(8,128)S(1)}, f32[136,256]{1,0:T(8,128)S(1)}, u32[]{:S(2)}, u32[]{:S(2)}) collective-permute-start(f32[136,256]{1,0:T(8,128)S(1)} %get-tuple-element.268), channel_id=1, source_target_pairs={{0,3},{1,2},{2,1},{3,0},{4,7},{5,6},{6,5},{7,4},{8,11},{9,10},{10,... | collective-permute-start | bytes 417800 | tf_op jit(solution)/shard_map/ppermute | solution.py:40
  (65 other events, 389.1 us)
Sparse Core Ops, SparseCore 0:
  10.8 28.4 all-gather.4
  40.9 24.6 all-gather.6
  205.3 67.1 all-gather.8
